TPU v7x, 512 devices: a whole 4x8x8 slice. The times are simulated.
512 devices in a mesh: section: 4 (over x), expert: 32 (over y_lo, z, core), dp: 4 (over y_hi).
Axes of the slice: x: 4, y: 8 (y_hi: 4, y_lo: 2; y = y_hi * 2 + y_lo), z: 8, core: 2. Of those that a mesh axis runs over, the one named last changes fastest.
Arguments:
- stream_in: bfloat16 [2, 2, 4096, 3584], P(None, None, ('expert', 'dp'), 'section'), may hold values from -6 to 6
- cotangent: bfloat16 [2, 2, 4096, 3584], P(None, None, ('expert', 'dp'), 'section'), may hold values from -6 to 6
- route_ids: int32 [2, 2, 2, 4096, 2], P(None, None, None, ('expert', 'dp')), may hold values from 0 to 31, all different within a row; in each aligned block of 32 rows (0 to 31, 32 to 63, ..., all dimensions but the last counted through in order) at most 4 rows name the same one
- route_gates: float32 [2, 2, 2, 4096, 2], P(None, None, None, ('expert', 'dp')), may hold values from 0.1 to 1
- norm_gain: float32 [2, 3584], replicated, may hold values from 0.25 to 1.75
- up_weight: bfloat16 [4, 32, 3584, 512], P('section', 'expert', 'dp'), may hold values from -0.09375 to 0.09375
- down_weight: bfloat16 [4, 32, 512, 3584], P('section', 'expert', None, 'dp'), may hold values from -0.1875 to 0.1875
Outputs:
- grad_up: bfloat16 [4, 32, 3584, 512], P('section', 'expert', 'dp')
- grad_down: bfloat16 [4, 32, 512, 3584], P('section', 'expert', None, 'dp')
Inputs may be any that keep to these rules, and one draw needn't show every extreme that they name: `route_ids`: each token names 2 different experts in each layer; among the tokens of one micro-batch of one device in one layer (aligned blocks of 32 rows) no expert is named more than 4 times, and some block names an expert exactly 4 times.
All inputs are finite; a program needn't handle non-finite values.
Results may differ from a plain program's by a relative error of at most 0.025.
Values may be sent and summed in bfloat16 or wider, within the bound.
A program may use at most 128 MiB of HBM per device.

v0:
```python
import jax
import jax.numpy as jnp
from jax import lax
from jax.sharding import PartitionSpec as P

EPSILON = 1e-06


def swapped(x, axis, distance):
    return lax.ppermute(x, axis, [(i, i ^ 1 << distance) for i in range(lax.axis_size(axis))])


def passed_along(block, axis, distance):
    devices = range(lax.axis_size(axis))
    route = [(i - distance, i) for i in devices if i - distance in devices]
    return lax.ppermute(block, axis, route)


def normalize(layer_in, gain_row):
    as_float = layer_in.astype(jnp.float32)
    scale_inv = lax.rsqrt(jnp.mean(as_float * as_float, axis=-1, keepdims=True) + EPSILON)
    return (as_float, scale_inv, (as_float * scale_inv * gain_row).astype(jnp.bfloat16))


def spread_matrix(chosen, capacity, peer_count):
    flat_ids = chosen.reshape(-1)
    matches = (flat_ids[:, None] == jnp.arange(peer_count, dtype=jnp.int32)[None, :]).astype(
        jnp.int32
    )
    earlier = jnp.cumsum(matches, axis=0) - matches
    position = jnp.sum(earlier * matches, axis=1)
    target = flat_ids * capacity + position
    slot_ids = jnp.arange(peer_count * capacity, dtype=jnp.int32)
    spread = (slot_ids[:, None] == target[None, :]).astype(jnp.bfloat16)
    return spread.reshape(peer_count, capacity, flat_ids.shape[0])


def swap_rows(block_rows):
    shape_now = block_rows.shape
    flat_rows = block_rows.reshape(shape_now[0] * shape_now[1], shape_now[2], shape_now[3])
    moved = lax.all_to_all(flat_rows, ("expert", "dp"), split_axis=0, concat_axis=0, tiled=True)
    return moved.reshape(shape_now)


def hidden_total(partial_value):
    return lax.psum(partial_value.astype(jnp.bfloat16), "dp").astype(jnp.float32)


def pair_total(partial_value):
    own_part = partial_value.astype(jnp.bfloat16)
    other_part = swapped(own_part, "section", 0)
    return (own_part.astype(jnp.float32) + other_part.astype(jnp.float32)).astype(jnp.bfloat16)


def hand_on(values, offset):
    return passed_along(values, "section", offset)


def plan(step_now, down_lead, up_lead, batches):
    down_offset = step_now - down_lead
    up_offset = step_now - up_lead
    is_down = jnp.mod(down_offset, 2) == 0
    offset = jnp.where(is_down, down_offset, up_offset)
    batch_pos = jnp.floor_divide(offset, 2)
    is_valid = (offset >= 0) & (batch_pos < batches)
    safe_pos = jnp.clip(batch_pos, 0, batches - 1)
    direction = jnp.where(is_down, 0, 1).astype(jnp.int32)
    return (is_down, is_valid, safe_pos, direction)


def put_masked(store, value, where_at, is_valid):
    old_value = lax.dynamic_index_in_dim(store, where_at, 0, keepdims=False)
    return lax.dynamic_update_index_in_dim(
        store, jnp.where(is_valid, value, old_value), where_at, 0
    )


def local(stream_in, cotangent, route_ids, route_gates, norm_gain, up_weight, down_weight):
    sections = lax.axis_size("section")
    places = sections // 2
    section_pos = lax.axis_index("section")
    place = section_pos // 2
    peer_count = lax.axis_size("expert")
    groups = lax.axis_size("dp")
    streams, cotans = (
        lax.all_gather(stream_in, "section", axis=3, tiled=True),
        lax.all_gather(cotangent, "section", axis=3, tiled=True),
    )
    w_up = up_weight[0, 0]
    w_down = down_weight[0, 0]
    gain_row = lax.dynamic_index_in_dim(norm_gain, place, 0, keepdims=False)
    routes = lax.dynamic_index_in_dim(route_ids, place, 0, keepdims=False)
    gate_raw = lax.dynamic_index_in_dim(route_gates, place, 0, keepdims=False)
    shares = gate_raw / jnp.sum(gate_raw, axis=-1, keepdims=True)
    batches = streams.shape[1]
    tokens_here = streams.shape[2]
    model_width = streams.shape[3]
    top_count = routes.shape[-1]
    part_width = w_up.shape[0]
    hidden = w_up.shape[1]
    capacity = min(tokens_here, max(2, 2 * tokens_here * top_count // peer_count))
    slot_count = peer_count * groups * capacity
    step_count = places + 2 * batches - 2
    pick_count = tokens_here * top_count
    contract_last = (((1,), (1,)), ((), ()))
    contract_first = (((0,), (0,)), ((), ()))

    def dispatch(spread, per_pick):
        blocks = per_pick.reshape(pick_count, groups, part_width)
        sent = jnp.einsum(
            "eca,agq->egcq", spread, blocks, preferred_element_type=jnp.float32
        ).astype(jnp.bfloat16)
        return swap_rows(sent).reshape(slot_count, part_width)

    def give_back(spread, rows_out):
        returned = swap_rows(rows_out.reshape(peer_count, groups, capacity, part_width))
        picked = jnp.einsum("eca,egcq->agq", spread, returned, preferred_element_type=jnp.float32)
        return picked.reshape(tokens_here, top_count, model_width)

    def picks_of(normed):
        return jnp.broadcast_to(normed[:, None, :], (tokens_here, top_count, model_width)).reshape(
            pick_count, model_width
        )

    zero_rows = jnp.zeros((tokens_here, model_width), jnp.bfloat16)
    inputs_kept = jnp.zeros((2 * batches, tokens_here, model_width), jnp.bfloat16)
    stores = (
        jnp.zeros((step_count, slot_count, part_width), jnp.bfloat16),
        jnp.zeros((step_count, slot_count, hidden), jnp.float32),
    )

    def forward_turn(step_now, state_in):
        from_below, from_above, kept_inputs, kept_rows = state_in
        is_down, is_valid, safe_pos, direction = plan(step_now, place, places - 1 - place, batches)
        at_entry = jnp.where(is_down, place == 0, place == places - 1)
        layer_in = jnp.where(
            at_entry, streams[direction, safe_pos], jnp.where(is_down, from_below, from_above)
        )
        chosen = routes[direction, safe_pos]
        share_now = shares[direction, safe_pos]
        as_float, scale_inv, normed = normalize(layer_in, gain_row)
        spread = spread_matrix(chosen, capacity, peer_count)
        received = dispatch(spread, picks_of(normed))
        pre_act = hidden_total(jnp.dot(received, w_up, preferred_element_type=jnp.float32))
        activated = jax.nn.silu(pre_act).astype(jnp.bfloat16)
        expert_out = pair_total(jnp.dot(activated, w_down, preferred_element_type=jnp.float32))
        picked = give_back(spread, expert_out)
        layer_out = (as_float + jnp.sum(share_now[:, :, None] * picked, axis=1)).astype(
            jnp.bfloat16
        )
        kept_slot = direction * batches + safe_pos
        kept_inputs = put_masked(kept_inputs, layer_in, kept_slot, is_valid)
        rows_kept, pre_kept = kept_rows
        kept_rows = (
            lax.dynamic_update_index_in_dim(rows_kept, received, step_now, 0),
            lax.dynamic_update_index_in_dim(pre_kept, pre_act, step_now, 0),
        )
        return (hand_on(layer_out, 2), hand_on(layer_out, -2), kept_inputs, kept_rows)

    state_out = lax.fori_loop(
        0, step_count, forward_turn, (zero_rows, zero_rows, inputs_kept, stores)
    )
    inputs_kept = state_out[2]
    stores = state_out[3]
    grad_stores = (
        jnp.zeros((step_count, slot_count, hidden), jnp.bfloat16),
        jnp.zeros((step_count, slot_count, part_width), jnp.bfloat16),
    )

    def backward_turn(step_now, state_in):
        cot_below, cot_above, kept_grads = state_in
        is_down, is_valid, safe_pos, direction = plan(step_now, places - 1 - place, place, batches)
        at_entry = jnp.where(is_down, place == places - 1, place == 0)
        incoming = jnp.where(
            at_entry, cotans[direction, safe_pos], jnp.where(is_down, cot_above, cot_below)
        )
        fwd_step = jnp.clip(
            jnp.where(is_down, place, places - 1 - place) + 2 * safe_pos, 0, step_count - 1
        )
        layer_in = lax.dynamic_index_in_dim(
            inputs_kept, direction * batches + safe_pos, 0, keepdims=False
        )
        chosen = routes[direction, safe_pos]
        share_now = shares[direction, safe_pos]
        as_float, scale_inv, normed = normalize(layer_in, gain_row)
        spread = spread_matrix(chosen, capacity, peer_count)
        incoming_f = incoming.astype(jnp.float32)
        out_grad = (
            (share_now[:, :, None] * incoming_f[:, None, :])
            .astype(jnp.bfloat16)
            .reshape(pick_count, model_width)
        )
        grad_recv = dispatch(spread, out_grad)
        pre_act = lax.dynamic_index_in_dim(stores[1], fwd_step, 0, keepdims=False)
        act_grad = hidden_total(
            lax.dot_general(grad_recv, w_down, contract_last, preferred_element_type=jnp.float32)
        )
        sigmoid_val = jax.nn.sigmoid(pre_act)
        pre_grad = (act_grad * sigmoid_val * (1.0 + pre_act * (1.0 - sigmoid_val))).astype(
            jnp.bfloat16
        )
        in_rows = pair_total(
            lax.dot_general(pre_grad, w_up, contract_last, preferred_element_type=jnp.float32)
        )
        normed_grad = jnp.sum(give_back(spread, in_rows), axis=1)
        scaled = normed_grad * gain_row
        layer_grad = (
            incoming_f
            + scale_inv * scaled
            - as_float * scale_inv**3 * jnp.mean(as_float * scaled, axis=-1, keepdims=True)
        )
        zero_bf = jnp.zeros((), jnp.bfloat16)
        masked_pre = jnp.where(is_valid, pre_grad, zero_bf)
        masked_out = jnp.where(is_valid, grad_recv, zero_bf)
        dz_kept, do_kept = kept_grads
        kept_grads = (
            put_masked(dz_kept, masked_pre, fwd_step, is_valid),
            put_masked(do_kept, masked_out, fwd_step, is_valid),
        )
        layer_back = layer_grad.astype(jnp.bfloat16)
        return (hand_on(layer_back, 2), hand_on(layer_back, -2), kept_grads)

    state_back = lax.fori_loop(0, step_count, backward_turn, (zero_rows, zero_rows, grad_stores))
    kept_grads = state_back[2]
    rows_all = stores[0].reshape(step_count * slot_count, part_width)
    act_all = jax.nn.silu(stores[1]).astype(jnp.bfloat16).reshape(step_count * slot_count, hidden)
    dz_all = kept_grads[0].reshape(step_count * slot_count, hidden)
    do_all = kept_grads[1].reshape(step_count * slot_count, part_width)
    grad_up = lax.dot_general(rows_all, dz_all, contract_first, preferred_element_type=jnp.float32)
    grad_down = lax.dot_general(act_all, do_all, contract_first, preferred_element_type=jnp.float32)
    return (grad_up.astype(jnp.bfloat16)[None, None], grad_down.astype(jnp.bfloat16)[None, None])


def solution(mesh):
    placed = (
        P(None, None, ("expert", "dp"), "section"),
        P(None, None, ("expert", "dp"), "section"),
        P(None, None, None, ("expert", "dp"), None),
        P(None, None, None, ("expert", "dp"), None),
        P(),
        P("section", "expert", "dp", None),
        P("section", "expert", None, "dp"),
    )
    return jax.shard_map(
        local,
        mesh=mesh,
        in_specs=placed,
        out_specs=(P("section", "expert", "dp", None), P("section", "expert", None, "dp")),
        check_vma=False,
    )
```

profile of v0, /device:TPU:6, one launch (start us, length us, event | category | flops | bytes accessed | tf_op | source)
XLA Modules:
  0.0 1486.0 jit_solution(3037326439255803674)
XLA Ops:
  32.1 705.9 %while.44 = (s32[]{:T(128)}, bf16[32,3584]{1,0:T(8,128)(2,1)S(1)}, bf16[32,3584]{1,0:T(8,128)(2,1)S(1)}, bf16[4,32,3584]{2,1,0:T(8,128)(2,1)}, bf16[4,512,896]{2...) while((s32[]{:T(128)}, bf16[32,3584]{1,0:T(8,128)(2,1)S(1)}, ...), condition=%wide.region_7.8_spmd, body=%wide.region_1.7_spmd.sunk | while | flops 1064071936 | bytes 45079936 | solution.py:160
  37.3 40.2 %all_to_all.52 = bf16[128,4,896]{2,1,0:T(4,128)(2,1)S(1)} all-to-all(bf16[128,4,896]{2,1,0:T(4,128)(2,1)S(1)} %bitcast.200), channel_id=1, replica_groups=mesh['section'=4,'expert'=32,'dp'=4] {'expert','dp'}, dimensions={0} | all-to-all | bytes 1835008 | tf_op jit(solution)/shard_map/while/body/eval_jaxpr/all_to_all | solution.py:41
  80.4 53.6 %all-reduce.3.cloned.1.call-done = bf16[512,512]{1,0:T(8,128)(2,1)} async-done(((bf16[512,512]{1,0:T(8,128)(2,1)}), bf16[512,512]{1,0:T(8,128)(2,1)}) %all-reduce.3.cloned.1.call-update) | async-done | bytes 524304 | tf_op jit(solution)/shard_map/while/body/eval_jaxpr/psum | solution.py:46
  174.5 25.0 %all-to-all-done.1 = bf16[128,4,896]{2,1,0:T(4,128)(2,1)S(1)} async-done(((bf16[128,4,896]{2,1,0:T(4,128)(2,1)}), bf16[128,4,896]{2,1,0:T(4,128)(2,1)S(1)}, u32[]{:S(2)}, u32[]{:S(2)}) %all-to-all-start.1) | async-done | bytes 917536 | tf_op jit(solution)/shard_map/while/body/eval_jaxpr/all_to_all | solution.py:41
  217.4 34.7 %all_to_all.52 = bf16[128,4,896]{2,1,0:T(4,128)(2,1)S(1)} all-to-all(bf16[128,4,896]{2,1,0:T(4,128)(2,1)S(1)} %bitcast.200), channel_id=1, replica_groups=mesh['section'=4,'expert'=32,'dp'=4] {'expert','dp'}, dimensions={0} | all-to-all | bytes 1835008 | tf_op jit(solution)/shard_map/while/body/eval_jaxpr/all_to_all | solution.py:41
  255.0 54.2 %all-reduce.3.cloned.1.call-done = bf16[512,512]{1,0:T(8,128)(2,1)} async-done(((bf16[512,512]{1,0:T(8,128)(2,1)}), bf16[512,512]{1,0:T(8,128)(2,1)}) %all-reduce.3.cloned.1.call-update) | async-done | bytes 524304 | tf_op jit(solution)/shard_map/while/body/eval_jaxpr/psum | solution.py:46
  349.8 25.0 %all-to-all-done.1 = bf16[128,4,896]{2,1,0:T(4,128)(2,1)S(1)} async-done(((bf16[128,4,896]{2,1,0:T(4,128)(2,1)}), bf16[128,4,896]{2,1,0:T(4,128)(2,1)S(1)}, u32[]{:S(2)}, u32[]{:S(2)}) %all-to-all-start.1) | async-done | bytes 917536 | tf_op jit(solution)/shard_map/while/body/eval_jaxpr/all_to_all | solution.py:41
  392.6 34.7 %all_to_all.52 = bf16[128,4,896]{2,1,0:T(4,128)(2,1)S(1)} all-to-all(bf16[128,4,896]{2,1,0:T(4,128)(2,1)S(1)} %bitcast.200), channel_id=1, replica_groups=mesh['section'=4,'expert'=32,'dp'=4] {'expert','dp'}, dimensions={0} | all-to-all | bytes 1835008 | tf_op jit(solution)/shard_map/while/body/eval_jaxpr/all_to_all | solution.py:41
  430.3 54.2 %all-reduce.3.cloned.1.call-done = bf16[512,512]{1,0:T(8,128)(2,1)} async-done(((bf16[512,512]{1,0:T(8,128)(2,1)}), bf16[512,512]{1,0:T(8,128)(2,1)}) %all-reduce.3.cloned.1.call-update) | async-done | bytes 524304 | tf_op jit(solution)/shard_map/while/body/eval_jaxpr/psum | solution.py:46
  524.8 25.2 %all-to-all-done.1 = bf16[128,4,896]{2,1,0:T(4,128)(2,1)S(1)} async-done(((bf16[128,4,896]{2,1,0:T(4,128)(2,1)}), bf16[128,4,896]{2,1,0:T(4,128)(2,1)S(1)}, u32[]{:S(2)}, u32[]{:S(2)}) %all-to-all-start.1) | async-done | bytes 917536 | tf_op jit(solution)/shard_map/while/body/eval_jaxpr/all_to_all | solution.py:41
  567.8 34.7 %all_to_all.52 = bf16[128,4,896]{2,1,0:T(4,128)(2,1)S(1)} all-to-all(bf16[128,4,896]{2,1,0:T(4,128)(2,1)S(1)} %bitcast.200), channel_id=1, replica_groups=mesh['section'=4,'expert'=32,'dp'=4] {'expert','dp'}, dimensions={0} | all-to-all | bytes 1835008 | tf_op jit(solution)/shard_map/while/body/eval_jaxpr/all_to_all | solution.py:41
  605.5 54.2 %all-reduce.3.cloned.1.call-done = bf16[512,512]{1,0:T(8,128)(2,1)} async-done(((bf16[512,512]{1,0:T(8,128)(2,1)}), bf16[512,512]{1,0:T(8,128)(2,1)}) %all-reduce.3.cloned.1.call-update) | async-done | bytes 524304 | tf_op jit(solution)/shard_map/while/body/eval_jaxpr/psum | solution.py:46
  700.1 25.2 %all-to-all-done.1 = bf16[128,4,896]{2,1,0:T(4,128)(2,1)S(1)} async-done(((bf16[128,4,896]{2,1,0:T(4,128)(2,1)}), bf16[128,4,896]{2,1,0:T(4,128)(2,1)S(1)}, u32[]{:S(2)}, u32[]{:S(2)}) %all-to-all-start.1) | async-done | bytes 917536 | tf_op jit(solution)/shard_map/while/body/eval_jaxpr/all_to_all | solution.py:41
  760.6 707.1 %while.45 = (s32[]{:T(128)}, bf16[32,3584]{1,0:T(8,128)(2,1)S(1)}, bf16[32,3584]{1,0:T(8,128)(2,1)}, bf16[4,512,512]{2,1,0:T(8,128)(2,1)}, bf16[4,512,896]{2,1,0...) while((s32[]{:T(128)}, bf16[32,3584]{1,0:T(8,128)(2,1)S(1)}, ...), condition=%wide.region_15.16_spmd, body=%wide.region_8.15_spmd.sunk | while | flops 1069609856 | bytes 57416420 | solution.py:223
  764.9 34.8 %all_to_all.53 = bf16[128,4,896]{2,1,0:T(4,128)(2,1)S(1)} all-to-all(bf16[128,4,896]{2,1,0:T(4,128)(2,1)S(1)} %bitcast.202), channel_id=1, replica_groups=mesh['section'=4,'expert'=32,'dp'=4] {'expert','dp'}, dimensions={0} | all-to-all | bytes 1835008 | tf_op jit(solution)/shard_map/while/body/eval_jaxpr/all_to_all | solution.py:41
  802.6 52.9 %all-reduce.5.cloned.1.call-done = bf16[512,512]{1,0:T(8,128)(2,1)} async-done(((bf16[512,512]{1,0:T(8,128)(2,1)}), bf16[512,512]{1,0:T(8,128)(2,1)}) %all-reduce.5.cloned.1.call-update) | async-done | bytes 524304 | tf_op jit(solution)/shard_map/while/body/eval_jaxpr/psum | solution.py:46
  940.5 34.9 %all_to_all.53 = bf16[128,4,896]{2,1,0:T(4,128)(2,1)S(1)} all-to-all(bf16[128,4,896]{2,1,0:T(4,128)(2,1)S(1)} %bitcast.202), channel_id=1, replica_groups=mesh['section'=4,'expert'=32,'dp'=4] {'expert','dp'}, dimensions={0} | all-to-all | bytes 1835008 | tf_op jit(solution)/shard_map/while/body/eval_jaxpr/all_to_all | solution.py:41
  978.3 54.4 %all-reduce.5.cloned.1.call-done = bf16[512,512]{1,0:T(8,128)(2,1)} async-done(((bf16[512,512]{1,0:T(8,128)(2,1)}), bf16[512,512]{1,0:T(8,128)(2,1)}) %all-reduce.5.cloned.1.call-update) | async-done | bytes 524304 | tf_op jit(solution)/shard_map/while/body/eval_jaxpr/psum | solution.py:46
  1076.4 22.2 %all-to-all-done.3 = bf16[128,4,896]{2,1,0:T(4,128)(2,1)S(1)} async-done(((bf16[128,4,896]{2,1,0:T(4,128)(2,1)}), bf16[128,4,896]{2,1,0:T(4,128)(2,1)S(1)}, u32[]{:S(2)}, u32[]{:S(2)}) %all-to-all-start.3) | async-done | bytes 917536 | tf_op jit(solution)/shard_map/while/body/eval_jaxpr/all_to_all | solution.py:41
  1117.8 34.8 %all_to_all.53 = bf16[128,4,896]{2,1,0:T(4,128)(2,1)S(1)} all-to-all(bf16[128,4,896]{2,1,0:T(4,128)(2,1)S(1)} %bitcast.202), channel_id=1, replica_groups=mesh['section'=4,'expert'=32,'dp'=4] {'expert','dp'}, dimensions={0} | all-to-all | bytes 1835008 | tf_op jit(solution)/shard_map/while/body/eval_jaxpr/all_to_all | solution.py:41
  1155.6 54.2 %all-reduce.5.cloned.1.call-done = bf16[512,512]{1,0:T(8,128)(2,1)} async-done(((bf16[512,512]{1,0:T(8,128)(2,1)}), bf16[512,512]{1,0:T(8,128)(2,1)}) %all-reduce.5.cloned.1.call-update) | async-done | bytes 524304 | tf_op jit(solution)/shard_map/while/body/eval_jaxpr/psum | solution.py:46
  1253.4 22.2 %all-to-all-done.3 = bf16[128,4,896]{2,1,0:T(4,128)(2,1)S(1)} async-done(((bf16[128,4,896]{2,1,0:T(4,128)(2,1)}), bf16[128,4,896]{2,1,0:T(4,128)(2,1)S(1)}, u32[]{:S(2)}, u32[]{:S(2)}) %all-to-all-start.3) | async-done | bytes 917536 | tf_op jit(solution)/shard_map/while/body/eval_jaxpr/all_to_all | solution.py:41
  1294.7 34.9 %all_to_all.53 = bf16[128,4,896]{2,1,0:T(4,128)(2,1)S(1)} all-to-all(bf16[128,4,896]{2,1,0:T(4,128)(2,1)S(1)} %bitcast.202), channel_id=1, replica_groups=mesh['section'=4,'expert'=32,'dp'=4] {'expert','dp'}, dimensions={0} | all-to-all | bytes 1835008 | tf_op jit(solution)/shard_map/while/body/eval_jaxpr/all_to_all | solution.py:41
  1332.5 54.4 %all-reduce.5.cloned.1.call-done = bf16[512,512]{1,0:T(8,128)(2,1)} async-done(((bf16[512,512]{1,0:T(8,128)(2,1)}), bf16[512,512]{1,0:T(8,128)(2,1)}) %all-reduce.5.cloned.1.call-update) | async-done | bytes 524304 | tf_op jit(solution)/shard_map/while/body/eval_jaxpr/psum | solution.py:46
  (401 shorter events, 609.7 us)
Async XLA Ops:
  32.1 101.9 %all-reduce.3.cloned.1.call-start = ((), (), s32[]{:S(2)}) async-start(), calls=%async_computation.4 | async-start | bytes 1048576 | tf_op jit(solution)/shard_map/while/body/eval_jaxpr/psum | solution.py:46
  136.1 22.7 %collective-permute-start = (bf16[512,896]{1,0:T(8,128)(2,1)S(1)}, bf16[512,896]{1,0:T(8,128)(2,1)S(1)}, u32[]{:S(2)}, u32[]{:S(2)}) collective-permute-start(bf16[512,896]{1,0:T(8,128)(2,1)S(1)} %convolution_convert_fusion.11), channel_id=1, source_target_pairs={{0,128},{128,0},{256,384},{384,256},{1,129},{129,1},{257,385},{385... | collective-permute-start | bytes 2752520 | tf_op jit(solution)/shard_map/while/body/eval_jaxpr/ppermute | solution.py:10
  160.1 39.5 %all-to-all-start.1 = ((bf16[128,4,896]{2,1,0:T(4,128)(2,1)}), bf16[128,4,896]{2,1,0:T(4,128)(2,1)S(1)}, u32[]{:S(2)}, u32[]{:S(2)}) async-start(bf16[128,4,896]{2,1,0:T(4,128)(2,1)} %reshape.349), calls=%async_computation.1 | async-start | bytes 1835008 | tf_op jit(solution)/shard_map/while/body/eval_jaxpr/all_to_all | solution.py:41
  212.3 97.0 %all-reduce.3.cloned.1.call-start = ((), (), s32[]{:S(2)}) async-start(), calls=%async_computation.4 | async-start | bytes 1048576 | tf_op jit(solution)/shard_map/while/body/eval_jaxpr/psum | solution.py:46
  311.3 22.7 %collective-permute-start = (bf16[512,896]{1,0:T(8,128)(2,1)S(1)}, bf16[512,896]{1,0:T(8,128)(2,1)S(1)}, u32[]{:S(2)}, u32[]{:S(2)}) collective-permute-start(bf16[512,896]{1,0:T(8,128)(2,1)S(1)} %convolution_convert_fusion.11), channel_id=1, source_target_pairs={{0,128},{128,0},{256,384},{384,256},{1,129},{129,1},{257,385},{385... | collective-permute-start | bytes 2752520 | tf_op jit(solution)/shard_map/while/body/eval_jaxpr/ppermute | solution.py:10
  335.3 39.5 %all-to-all-start.1 = ((bf16[128,4,896]{2,1,0:T(4,128)(2,1)}), bf16[128,4,896]{2,1,0:T(4,128)(2,1)S(1)}, u32[]{:S(2)}, u32[]{:S(2)}) async-start(bf16[128,4,896]{2,1,0:T(4,128)(2,1)} %reshape.349), calls=%async_computation.1 | async-start | bytes 1835008 | tf_op jit(solution)/shard_map/while/body/eval_jaxpr/all_to_all | solution.py:41
  387.5 97.0 %all-reduce.3.cloned.1.call-start = ((), (), s32[]{:S(2)}) async-start(), calls=%async_computation.4 | async-start | bytes 1048576 | tf_op jit(solution)/shard_map/while/body/eval_jaxpr/psum | solution.py:46
  486.5 22.7 %collective-permute-start = (bf16[512,896]{1,0:T(8,128)(2,1)S(1)}, bf16[512,896]{1,0:T(8,128)(2,1)S(1)}, u32[]{:S(2)}, u32[]{:S(2)}) collective-permute-start(bf16[512,896]{1,0:T(8,128)(2,1)S(1)} %convolution_convert_fusion.11), channel_id=1, source_target_pairs={{0,128},{128,0},{256,384},{384,256},{1,129},{129,1},{257,385},{385... | collective-permute-start | bytes 2752520 | tf_op jit(solution)/shard_map/while/body/eval_jaxpr/ppermute | solution.py:10
  510.5 39.5 %all-to-all-start.1 = ((bf16[128,4,896]{2,1,0:T(4,128)(2,1)}), bf16[128,4,896]{2,1,0:T(4,128)(2,1)S(1)}, u32[]{:S(2)}, u32[]{:S(2)}) async-start(bf16[128,4,896]{2,1,0:T(4,128)(2,1)} %reshape.349), calls=%async_computation.1 | async-start | bytes 1835008 | tf_op jit(solution)/shard_map/while/body/eval_jaxpr/all_to_all | solution.py:41
  562.7 97.0 %all-reduce.3.cloned.1.call-start = ((), (), s32[]{:S(2)}) async-start(), calls=%async_computation.4 | async-start | bytes 1048576 | tf_op jit(solution)/shard_map/while/body/eval_jaxpr/psum | solution.py:46
  661.8 22.6 %collective-permute-start = (bf16[512,896]{1,0:T(8,128)(2,1)S(1)}, bf16[512,896]{1,0:T(8,128)(2,1)S(1)}, u32[]{:S(2)}, u32[]{:S(2)}) collective-permute-start(bf16[512,896]{1,0:T(8,128)(2,1)S(1)} %convolution_convert_fusion.11), channel_id=1, source_target_pairs={{0,128},{128,0},{256,384},{384,256},{1,129},{129,1},{257,385},{385... | collective-permute-start | bytes 2752520 | tf_op jit(solution)/shard_map/while/body/eval_jaxpr/ppermute | solution.py:10
  685.8 39.5 %all-to-all-start.1 = ((bf16[128,4,896]{2,1,0:T(4,128)(2,1)}), bf16[128,4,896]{2,1,0:T(4,128)(2,1)S(1)}, u32[]{:S(2)}, u32[]{:S(2)}) async-start(bf16[128,4,896]{2,1,0:T(4,128)(2,1)} %reshape.349), calls=%async_computation.1 | async-start | bytes 1835008 | tf_op jit(solution)/shard_map/while/body/eval_jaxpr/all_to_all | solution.py:41
  760.6 94.9 %all-reduce.5.cloned.1.call-start = ((), (), s32[]{:S(2)}) async-start(), calls=%async_computation.5 | async-start | bytes 1048576 | tf_op jit(solution)/shard_map/while/body/eval_jaxpr/psum | solution.py:46
  857.9 22.7 %collective-permute-start.3 = (bf16[512,896]{1,0:T(8,128)(2,1)S(1)}, bf16[512,896]{1,0:T(8,128)(2,1)S(1)}, u32[]{:S(2)}, u32[]{:S(2)}) collective-permute-start(bf16[512,896]{1,0:T(8,128)(2,1)S(1)} %convolution_convert_fusion.13), channel_id=1, source_target_pairs={{0,128},{128,0},{256,384},{384,256},{1,129},{129,1},{257,385},{385... | collective-permute-start | bytes 2752520 | tf_op jit(solution)/shard_map/while/body/eval_jaxpr/ppermute | solution.py:10
  881.9 39.5 %all-to-all-start.3 = ((bf16[128,4,896]{2,1,0:T(4,128)(2,1)}), bf16[128,4,896]{2,1,0:T(4,128)(2,1)S(1)}, u32[]{:S(2)}, u32[]{:S(2)}) async-start(bf16[128,4,896]{2,1,0:T(4,128)(2,1)} %reshape.352), calls=%async_computation.3 | async-start | bytes 1835008 | tf_op jit(solution)/shard_map/while/body/eval_jaxpr/all_to_all | solution.py:41
  936.3 96.4 %all-reduce.5.cloned.1.call-start = ((), (), s32[]{:S(2)}) async-start(), calls=%async_computation.5 | async-start | bytes 1048576 | tf_op jit(solution)/shard_map/while/body/eval_jaxpr/psum | solution.py:46
  1035.1 22.6 %collective-permute-start.3 = (bf16[512,896]{1,0:T(8,128)(2,1)S(1)}, bf16[512,896]{1,0:T(8,128)(2,1)S(1)}, u32[]{:S(2)}, u32[]{:S(2)}) collective-permute-start(bf16[512,896]{1,0:T(8,128)(2,1)S(1)} %convolution_convert_fusion.13), channel_id=1, source_target_pairs={{0,128},{128,0},{256,384},{384,256},{1,129},{129,1},{257,385},{385... | collective-permute-start | bytes 2752520 | tf_op jit(solution)/shard_map/while/body/eval_jaxpr/ppermute | solution.py:10
  1059.1 39.5 %all-to-all-start.3 = ((bf16[128,4,896]{2,1,0:T(4,128)(2,1)}), bf16[128,4,896]{2,1,0:T(4,128)(2,1)S(1)}, u32[]{:S(2)}, u32[]{:S(2)}) async-start(bf16[128,4,896]{2,1,0:T(4,128)(2,1)} %reshape.352), calls=%async_computation.3 | async-start | bytes 1835008 | tf_op jit(solution)/shard_map/while/body/eval_jaxpr/all_to_all | solution.py:41
  1113.5 96.2 %all-reduce.5.cloned.1.call-start = ((), (), s32[]{:S(2)}) async-start(), calls=%async_computation.5 | async-start | bytes 1048576 | tf_op jit(solution)/shard_map/while/body/eval_jaxpr/psum | solution.py:46
  1212.1 22.7 %collective-permute-start.3 = (bf16[512,896]{1,0:T(8,128)(2,1)S(1)}, bf16[512,896]{1,0:T(8,128)(2,1)S(1)}, u32[]{:S(2)}, u32[]{:S(2)}) collective-permute-start(bf16[512,896]{1,0:T(8,128)(2,1)S(1)} %convolution_convert_fusion.13), channel_id=1, source_target_pairs={{0,128},{128,0},{256,384},{384,256},{1,129},{129,1},{257,385},{385... | collective-permute-start | bytes 2752520 | tf_op jit(solution)/shard_map/while/body/eval_jaxpr/ppermute | solution.py:10
  1236.2 39.5 %all-to-all-start.3 = ((bf16[128,4,896]{2,1,0:T(4,128)(2,1)}), bf16[128,4,896]{2,1,0:T(4,128)(2,1)S(1)}, u32[]{:S(2)}, u32[]{:S(2)}) async-start(bf16[128,4,896]{2,1,0:T(4,128)(2,1)} %reshape.352), calls=%async_computation.3 | async-start | bytes 1835008 | tf_op jit(solution)/shard_map/while/body/eval_jaxpr/all_to_all | solution.py:41
  1290.6 96.4 %all-reduce.5.cloned.1.call-start = ((), (), s32[]{:S(2)}) async-start(), calls=%async_computation.5 | async-start | bytes 1048576 | tf_op jit(solution)/shard_map/while/body/eval_jaxpr/psum | solution.py:46
  1389.3 22.6 %collective-permute-start.3 = (bf16[512,896]{1,0:T(8,128)(2,1)S(1)}, bf16[512,896]{1,0:T(8,128)(2,1)S(1)}, u32[]{:S(2)}, u32[]{:S(2)}) collective-permute-start(bf16[512,896]{1,0:T(8,128)(2,1)S(1)} %convolution_convert_fusion.13), channel_id=1, source_target_pairs={{0,128},{128,0},{256,384},{384,256},{1,129},{129,1},{257,385},{385... | collective-permute-start | bytes 2752520 | tf_op jit(solution)/shard_map/while/body/eval_jaxpr/ppermute | solution.py:10
  1413.3 39.5 %all-to-all-start.3 = ((bf16[128,4,896]{2,1,0:T(4,128)(2,1)}), bf16[128,4,896]{2,1,0:T(4,128)(2,1)S(1)}, u32[]{:S(2)}, u32[]{:S(2)}) async-start(bf16[128,4,896]{2,1,0:T(4,128)(2,1)} %reshape.352), calls=%async_computation.3 | async-start | bytes 1835008 | tf_op jit(solution)/shard_map/while/body/eval_jaxpr/all_to_all | solution.py:41
  (30 other events, 834.4 us)
Sparse Core Ops, SparseCore 0:
  80.5 53.4 all-reduce.2
  255.2 54.0 all-reduce.2
  430.4 53.9 all-reduce.2
  605.6 54.0 all-reduce.2
  802.8 52.7 all-reduce.4
  978.4 54.2 all-reduce.4
  1155.7 54.0 all-reduce.4
  1332.6 54.2 all-reduce.4
where the time goes:
time: 1490 us
  waiting for transfers between devices  795 us (53%)
  blocking collectives  321 us (22%)
  starting transfers between devices  182 us (12%)
  local copies, waits for them, and re-layouts  59.6 us (4%)
  matrix products  57.7 us (4%)
  other arithmetic  54.6 us (4%)
    psum x8, waiting for transfers between devices, hidden_total(): lax.psum(partial_value.astype(jnp.bfloat16), 'dp').astype(jnp.float32)  432 us
    all_to_all x8, blocking collectives, swap_rows(): lax.all_to_all(flat_rows, ('expert', 'dp'), split_axis=0, concat_axis=0,...  284 us
    all_to_all x8, waiting for transfers between devices, swap_rows(): lax.all_to_all(flat_rows, ('expert', 'dp'), split_axis=0, concat_axis=0,...  189 us
    ppermute x8, waiting for transfers between devices, swapped(): lax.ppermute(x, axis, [(i, i ^ 1 << distance) for i in range(lax.axis_siz...  159 us
    all_to_all x8, starting transfers between devices, swap_rows(): lax.all_to_all(flat_rows, ('expert', 'dp'), split_axis=0, concat_axis=0,...  98 us
    ppermute x16, starting transfers between devices, passed_along(): return lax.ppermute(block, axis, route)  61.7 us
  transfers between devices with their start and end apart: 40, of which 36 were waited for; matrix products, arithmetic and copies ran while one was open for 3% of the time, Pallas kernels for 0%

commit v1 on v0

v1 whole, which is shorter than its diff:
```python
import jax
import jax.numpy as jnp
from jax import lax
from jax.experimental import pallas as pl
from jax.experimental.pallas import tpu as pltpu
from jax.sharding import PartitionSpec as P

EPSILON = 1e-06
MESH = pl.DeviceIdType.MESH
F32 = jnp.float32
BF16 = jnp.bfloat16
EXPERTS = 32
GROUPS = 4
TOKENS = 256
MSG = 16
SLOTS = EXPERTS * MSG
PART = 896
HALF = 512
CHUNKS = 2
CROWS = SLOTS // CHUNKS
QUART = CROWS // GROUPS
CPEERS = EXPERTS // CHUNKS
VMEM_LIMIT = 56 * 1024 * 1024


def dot(a, b):
    return lax.dot_general(a, b, (((1,), (0,)), ((), ())), preferred_element_type=F32)


def dot_t(a, b):
    return lax.dot_general(a, b, (((1,), (1,)), ((), ())), preferred_element_type=F32)


def t_dot(a, b):
    return lax.dot_general(a, b, (((0,), (0,)), ((), ())), preferred_element_type=F32)


def copy_to(src, dst, send_sem, recv_sem, device):
    return pltpu.make_async_remote_copy(
        src_ref=src,
        dst_ref=dst,
        send_sem=send_sem,
        recv_sem=recv_sem,
        device_id=device,
        device_id_type=MESH,
    )


class Place:
    def __init__(self):
        self.section = lax.axis_index("section")
        self.expert = lax.axis_index("expert")
        self.group = lax.axis_index("dp")
        self.half = self.section % 2
        self.pair = self.section // 2
        self.partner = self.section + 1 - 2 * self.half


def greet_experts(here, barrier):
    def one(k, carry):
        pl.semaphore_signal(
            barrier,
            inc=1,
            device_id={"expert": (here.expert + k) % EXPERTS},
            device_id_type=MESH,
        )
        return carry

    lax.fori_loop(1, EXPERTS, one, 0)


def greet(barrier, device):
    pl.semaphore_signal(barrier, inc=1, device_id=device, device_id_type=MESH)


class Exchange:
    def __init__(self, here, src, dst, sems, sign):
        self.here, self.src, self.dst, self.sems, self.sign = here, src, dst, sems, sign

    def copy(self, k):
        rows = pl.ds(pl.multiple_of(k * MSG, MSG), MSG)
        peer = (self.here.expert + self.sign * k + EXPERTS) % EXPERTS
        return copy_to(
            self.src.at[rows],
            self.dst.at[rows],
            self.sems.at[0, k],
            self.sems.at[1, k],
            {"expert": peer},
        )

    def start(self, low=0, high=EXPERTS):
        if low == 0:
            self.dst[0:MSG] = self.src[0:MSG]

        def one(k, carry):
            self.copy(k).start()
            return carry

        lax.fori_loop(max(low, 1), high, one, 0)

    def wait_recv(self, low=0, high=EXPERTS):
        def one(k, carry):
            self.copy(k).wait_recv()
            return carry

        lax.fori_loop(max(low, 1), high, one, 0)

    def wait_send(self):
        def one(k, carry):
            self.copy(k).wait_send()
            return carry

        lax.fori_loop(1, EXPERTS, one, 0)


class GroupSum:
    def __init__(self, here, parts, landed, sems):
        self.here, self.parts, self.landed, self.sems = here, parts, landed, sems

    def copy(self, c, j):
        peer = (self.here.group + j) % GROUPS
        rows = pl.ds(pl.multiple_of(c * CROWS + peer * QUART, QUART), QUART)
        return copy_to(
            self.parts.at[rows],
            self.landed.at[c, j - 1],
            self.sems.at[0, c, j - 1],
            self.sems.at[1, c, j - 1],
            {"dp": peer},
        )

    def start(self, c):
        for j in (2, 1, 3):
            self.copy(c, j).start()

    def total(self, c):
        for j in (1, 3, 2):
            self.copy(c, j).wait_recv()
        rows = pl.ds(pl.multiple_of(c * CROWS + self.here.group * QUART, QUART), QUART)
        value = self.parts[rows].astype(F32)
        for j in (1, 2, 3):
            value = value + self.landed[c, j - 1].astype(F32)
        return value

    def wait_send(self):
        for c in range(CHUNKS):
            for j in (1, 2, 3):
                self.copy(c, j).wait_send()


class GroupGather:
    def __init__(self, here, whole, sems):
        self.here, self.whole, self.sems = here, whole, sems

    def rows(self, c, j):
        quarter = (self.here.group + GROUPS - j) % GROUPS
        return pl.ds(pl.multiple_of(c * CROWS + quarter * QUART, QUART), QUART)

    def copy(self, c, j, owner):
        where = self.whole.at[self.rows(c, owner)]
        return copy_to(
            where,
            where,
            self.sems.at[0, c, j - 1],
            self.sems.at[1, c, j - 1],
            {"dp": (self.here.group + j) % GROUPS},
        )

    def put(self, c, value):
        self.whole[self.rows(c, 0)] = value

    def start(self, c):
        for j in (2, 1, 3):
            self.copy(c, j, 0).start()

    def wait_recv(self, c):
        for j in (1, 3, 2):
            self.copy(c, j, j).wait_recv()

    def wait_send(self):
        for c in range(CHUNKS):
            for j in (1, 2, 3):
                self.copy(c, j, 0).wait_send()


class TokenSum:
    def __init__(self, here, own, landed, sems):
        self.here, self.own, self.landed, self.sems = here, own, landed, sems

    def copy(self, j):
        return copy_to(
            self.own,
            self.landed.at[j - 1],
            self.sems.at[0, j - 1],
            self.sems.at[1, j - 1],
            {"dp": (self.here.group + j) % GROUPS},
        )

    def start(self, column):
        self.own[...] = jnp.broadcast_to(column, (TOKENS, 128)).T[0:8]
        for j in (2, 1, 3):
            self.copy(j).start()

    def total(self):
        for j in (1, 3, 2):
            self.copy(j).wait_recv()
        value = self.own[...] + self.landed[0] + self.landed[1] + self.landed[2]
        return jnp.broadcast_to(value[0:1], (128, TOKENS)).T[:, 0:1]

    def wait_send(self):
        for j in (1, 2, 3):
            self.copy(j).wait_send()


def picks_by_slot(slot_row):
    slots = lax.broadcasted_iota(jnp.int32, (SLOTS, TOKENS), 0)
    return slots == slot_row[0:1], slots == slot_row[1:2]


def spread_of(slot_row):
    first, second = picks_by_slot(slot_row)
    return jnp.where(first | second, 1.0, 0.0).astype(BF16)


def shares_by_slot(slot_row, share_row):
    first, second = picks_by_slot(slot_row)
    return jnp.where(first, share_row[0:1], 0.0) + jnp.where(second, share_row[1:2], 0.0)


def picks_by_token(slot_col):
    slots = lax.broadcasted_iota(jnp.int32, (TOKENS, SLOTS), 1)
    return slots == slot_col[:, 0:1], slots == slot_col[:, 1:2]


def collect_of(slot_col):
    first, second = picks_by_token(slot_col)
    return jnp.where(first | second, 1.0, 0.0).astype(BF16)


def shares_by_token(slot_col, share_col):
    first, second = picks_by_token(slot_col)
    return jnp.where(first, share_col[:, 0:1], 0.0) + jnp.where(second, share_col[:, 1:2], 0.0)


def exact_dot(weights, values):
    high = weights.astype(BF16)
    low = (weights - high.astype(F32)).astype(BF16)
    return dot(high, values) + dot(low, values)


def up_parts(rows, up, up_other, parts, c):
    at = pl.ds(c * CROWS, CROWS)
    parts[at, 0:HALF] = dot(rows[at], up[...]).astype(BF16)
    parts[at, HALF:] = dot(rows[at], up_other[...]).astype(BF16)


def down_parts(rows, down, down_other, parts, c):
    at = pl.ds(c * CROWS, CROWS)
    parts[at, 0:HALF] = dot_t(rows[at], down[...]).astype(BF16)
    parts[at, HALF:] = dot_t(rows[at], down_other[...]).astype(BF16)


def norm_scale(total):
    return lax.rsqrt(total * (1.0 / (GROUPS * PART)) + EPSILON)


def pre_gradient(act_grad, pre):
    gate = jax.nn.sigmoid(pre)
    return (act_grad * gate * (1.0 + pre * (1.0 - gate))).astype(BF16)


def first_forward(
    stream, cotangent, up, down, gain, slot_row, slot_col, share_col,
    rows, pre, act, handed, cotan, up_other, down_other,
    layer_in, send, parts, landed, out, back, leaving, token_own, token_landed,
    stream_sems, cotan_sems, pair_sems, token_sems, go_sems, sum_sems, gather_sems, back_sems, hand_sems,
):
    here = Place()
    barrier = pltpu.get_barrier_semaphore()
    greet_experts(here, barrier)

    def greet_other(i, carry):
        at = (here.section * GROUPS + here.group + i) % 16
        greet(barrier, {"section": at // GROUPS, "dp": at % GROUPS})
        return carry

    lax.fori_loop(1, 16, greet_other, 0)
    pl.semaphore_wait(barrier, EXPERTS - 1 + 15)

    def cut_copy(source, target, sems, section, owner):
        return copy_to(
            source, target.at[owner], sems.at[0, section], sems.at[1, owner],
            {"section": section, "dp": here.section},
        )

    def send_cut(source, target, sems, flip):
        for section in range(4):
            direction = section // 2 if not flip else 1 - section // 2
            stays = (here.section == section) & (here.group == section)

            @pl.when(stays)
            def _():
                target[pl.ds(here.group, 1)] = source[direction : direction + 1]

            @pl.when(jnp.logical_not(stays))
            def _():
                cut_copy(source.at[direction], target, sems, section, here.group).start()

    def wait_cut(source, target, sems, recv):
        for i in range(4):
            if recv:
                stays = (here.section == here.group) & (here.group == i)
            else:
                stays = (here.section == i) & (here.group == i)

            @pl.when(jnp.logical_not(stays))
            def _():
                if recv:
                    cut_copy(source.at[0], target, sems, 0, i).wait_recv()
                else:
                    cut_copy(source.at[0], target, sems, i, here.group).wait_send()

    send_cut(stream, layer_in, stream_sems, False)
    to_partner = {"section": here.partner}
    up_copy = copy_to(up, up_other, pair_sems.at[0, 0], pair_sems.at[1, 0], to_partner)
    down_copy = copy_to(down, down_other, pair_sems.at[0, 1], pair_sems.at[1, 1], to_partner)
    up_copy.start()

    wait_cut(stream, layer_in, stream_sems, True)
    token_sum = TokenSum(here, token_own, token_landed, token_sems)
    values = layer_in[...].reshape(TOKENS, PART).astype(F32)
    token_sum.start(jnp.sum(values * values, axis=1, keepdims=True))
    spread = spread_of(slot_row[...])
    scale = norm_scale(token_sum.total())
    normed = (values * scale * gain[...]).astype(BF16)
    send[...] = dot(spread, normed).astype(BF16)
    go = Exchange(here, send, rows, go_sems, 1)
    go.start()
    down_copy.start()
    send_cut(cotangent, cotan, cotan_sems, True)

    group_sum = GroupSum(here, parts, landed, sum_sems)
    gather = GroupGather(here, act, gather_sems)
    go_back = Exchange(here, out, back, back_sems, -1)
    up_copy.wait_recv()
    for c in range(CHUNKS):
        go.wait_recv(c * CPEERS, (c + 1) * CPEERS)
        up_parts(rows, up, up_other, parts, c)
        group_sum.start(c)
    for c in range(CHUNKS):
        total = group_sum.total(c)
        pre[c] = total
        gather.put(c, (total * jax.nn.sigmoid(total)).astype(BF16))
        gather.start(c)
    down_copy.wait_recv()
    for c in range(CHUNKS):
        gather.wait_recv(c)
        at = pl.ds(c * CROWS, CROWS)
        made = dot(act[at, 0:HALF], down[...]) + dot(act[at, HALF:], down_other[...])
        out[at] = made.astype(BF16)
        go_back.start(c * CPEERS, (c + 1) * CPEERS)
    weights = shares_by_token(slot_col[...], share_col[...])
    go_back.wait_recv()
    residual = layer_in[...].reshape(TOKENS, PART).astype(F32) * (1 - here.half).astype(F32)
    leaving[...] = (residual + exact_dot(weights, back[...])).astype(BF16)
    hand_on(here, leaving, handed, hand_sems)

    wait_cut(cotangent, cotan, cotan_sems, True)
    wait_cut(stream, layer_in, stream_sems, False)
    wait_cut(cotangent, cotan, cotan_sems, False)
    up_copy.wait_send()
    down_copy.wait_send()
    token_sum.wait_send()
    go.wait_send()
    group_sum.wait_send()
    gather.wait_send()
    go_back.wait_send()


def hand_on(here, leaving, handed, sems):
    def one(j, owner):
        return copy_to(
            leaving, handed.at[owner], sems.at[0, j], sems.at[1, owner],
            {"section": 2 * (1 - here.pair) + j},
        )

    for j in range(2):
        one(j, here.half).start()
    for j in range(2):
        one(0, j).wait_recv()
    for j in range(2):
        one(j, here.half).wait_send()


def greet_near(here, barrier, other_pair, partner):
    greet_experts(here, barrier)
    for j in (1, 2, 3):
        greet(barrier, {"dp": (here.group + j) % GROUPS})
    count = EXPERTS - 1 + 3
    if other_pair:
        for j in range(2):
            greet(barrier, {"section": 2 * (1 - here.pair) + j})
        count += 2
    if partner:
        greet(barrier, {"section": here.partner})
        count += 1
    pl.semaphore_wait(barrier, count)


def second_layer(
    handed, cotan, up, up_other, down, down_other, gain, slot_row, slot_col, share_row,
    rows, act, grads, pre_grad, handed_back,
    send, send_grads, parts, landed, grad_parts, grad_landed, out, back, leaving,
    token_own, token_landed, mix_own, mix_landed,
    token_sems, mix_sems, go_sems, grad_sems, sum_sems, grad_sum_sems, gather_sems, act_sems, back_sems, hand_sems,
):
    here = Place()
    greet_near(here, pltpu.get_barrier_semaphore(), True, False)

    def layer_in():
        return (handed[0].astype(F32) + handed[1].astype(F32)).astype(BF16).astype(F32)

    token_sum = TokenSum(here, token_own, token_landed, token_sems)
    values = layer_in()
    token_sum.start(jnp.sum(values * values, axis=1, keepdims=True))
    spread = spread_of(slot_row[...])
    shares = shares_by_slot(slot_row[...], share_row[...])
    send_grads[...] = exact_dot(shares, cotan[...].reshape(TOKENS, PART)).astype(BF16)
    scale = norm_scale(token_sum.total())
    normed = (layer_in() * scale * gain[...]).astype(BF16)
    send[...] = dot(spread, normed).astype(BF16)
    go = Exchange(here, send, rows, go_sems, 1)
    go_grads = Exchange(here, send_grads, grads, grad_sems, 1)
    go.start()
    go_grads.start()

    group_sum = GroupSum(here, parts, landed, sum_sems)
    grad_sum = GroupSum(here, grad_parts, grad_landed, grad_sum_sems)
    gather = GroupGather(here, pre_grad, gather_sems)
    act_gather = GroupGather(here, act, act_sems)
    go_back = Exchange(here, out, back, back_sems, -1)
    for c in range(CHUNKS):
        go.wait_recv(c * CPEERS, (c + 1) * CPEERS)
        up_parts(rows, up, up_other, parts, c)
        group_sum.start(c)
    for c in range(CHUNKS):
        go_grads.wait_recv(c * CPEERS, (c + 1) * CPEERS)
        down_parts(grads, down, down_other, grad_parts, c)
        grad_sum.start(c)
    for c in range(CHUNKS):
        pre = group_sum.total(c)
        act_gather.put(c, (pre * jax.nn.sigmoid(pre)).astype(BF16))
        gather.put(c, pre_gradient(grad_sum.total(c), pre))
        gather.start(c)
    for c in range(CHUNKS):
        gather.wait_recv(c)
        at = pl.ds(c * CROWS, CROWS)
        made = dot_t(pre_grad[at, 0:HALF], up[...]) + dot_t(pre_grad[at, HALF:], up_other[...])
        out[at] = made.astype(BF16)
        go_back.start(c * CPEERS, (c + 1) * CPEERS)
    for c in range(CHUNKS):
        act_gather.start(c)
    collect = collect_of(slot_col[...])
    go_back.wait_recv()
    scaled = dot(collect, back[...]) * gain[...]
    mix = TokenSum(here, mix_own, mix_landed, mix_sems)
    mix.start(jnp.sum(layer_in() * scaled, axis=1, keepdims=True))
    direct = cotan[...].reshape(TOKENS, PART).astype(F32) * (1 - here.half).astype(F32)
    direct = direct + scale * scaled
    mean = mix.total() * (1.0 / (GROUPS * PART))
    leaving[...] = (direct - layer_in() * (scale * scale * scale * mean)).astype(BF16)
    hand_on(here, leaving, handed_back, hand_sems)

    for c in range(CHUNKS):
        act_gather.wait_recv(c)
    token_sum.wait_send()
    mix.wait_send()
    go.wait_send()
    go_grads.wait_send()
    group_sum.wait_send()
    grad_sum.wait_send()
    gather.wait_send()
    act_gather.wait_send()
    go_back.wait_send()


def first_backward(
    handed_back, down, down_other, slot_row, share_row, rows1, act1, pre1, rows2, act2, grads2, pre_grad2,
    grad_up, grad_down,
    send, grads1, pre_grad1, parts, landed, sum_up, sum_down, give_up, give_down, got_up, got_down,
    go_sems, sum_sems, gather_sems, pair_sems,
):
    here = Place()
    greet_near(here, pltpu.get_barrier_semaphore(), False, True)
    incoming = (handed_back[0].astype(F32) + handed_back[1].astype(F32)).astype(BF16)
    send[...] = exact_dot(shares_by_slot(slot_row[...], share_row[...]), incoming).astype(BF16)
    go = Exchange(here, send, grads1, go_sems, 1)
    go.start()

    @pl.loop(0, PART // 128)
    def _(i):
        at = pl.ds(pl.multiple_of(i * 128, 128), 128)
        sum_up[at] = t_dot(rows2[:, at], pre_grad2[...])

    @pl.loop(0, 2 * HALF // 128)
    def _(i):
        at = pl.ds(pl.multiple_of(i * 128, 128), 128)
        sum_down[at] = t_dot(act2[:, at], grads2[...])

    group_sum = GroupSum(here, parts, landed, sum_sems)
    gather = GroupGather(here, pre_grad1, gather_sems)
    to_partner = {"section": here.partner}
    down_copy = copy_to(give_down, got_down, pair_sems.at[0, 0], pair_sems.at[1, 0], to_partner)
    up_copy = copy_to(give_up, got_up, pair_sems.at[0, 1], pair_sems.at[1, 1], to_partner)
    for c in range(CHUNKS):
        go.wait_recv(c * CPEERS, (c + 1) * CPEERS)
        down_parts(grads1, down, down_other, parts, c)
        group_sum.start(c)

    @pl.loop(0, HALF // 128)
    def _(i):
        at = pl.ds(pl.multiple_of(i * 128, 128), 128)
        far = pl.ds(pl.multiple_of(HALF + i * 128, 128), 128)
        give_down[at] = (sum_down[far] + t_dot(act1[:, far], grads1[...])).astype(BF16)

    down_copy.start()
    for c in range(CHUNKS):
        gather.put(c, pre_gradient(group_sum.total(c), pre1[c]))
        gather.start(c)

    @pl.loop(0, HALF // 128)
    def _(i):
        at = pl.ds(pl.multiple_of(i * 128, 128), 128)
        sum_down[at] += t_dot(act1[:, at], grads1[...])

    for c in range(CHUNKS):
        gather.wait_recv(c)

    @pl.loop(0, PART // 128)
    def _(i):
        at = pl.ds(pl.multiple_of(i * 128, 128), 128)
        give_up[at] = (sum_up[at, HALF:] + t_dot(rows1[:, at], pre_grad1[:, HALF:])).astype(BF16)

    up_copy.start()

    @pl.loop(0, PART // 128)
    def _(i):
        at = pl.ds(pl.multiple_of(i * 128, 128), 128)
        sum_up[at, 0:HALF] += t_dot(rows1[:, at], pre_grad1[:, 0:HALF])

    down_copy.wait_recv()
    grad_down[...] = (sum_down[0:HALF] + got_down[...].astype(F32)).astype(BF16)
    up_copy.wait_recv()
    grad_up[...] = (sum_up[:, 0:HALF] + got_up[...].astype(F32)).astype(BF16)
    down_copy.wait_send()
    up_copy.wait_send()
    go.wait_send()
    group_sum.wait_send()
    gather.wait_send()


def call(kernel, collective_id, outs, scratch, *operands):
    whole = pl.BlockSpec(memory_space=pltpu.VMEM)
    return pl.pallas_call(
        kernel,
        out_shape=[jax.ShapeDtypeStruct(shape, dtype) for shape, dtype in outs],
        in_specs=[whole] * len(operands),
        out_specs=[whole] * len(outs),
        scratch_shapes=scratch,
        compiler_params=pltpu.CompilerParams(
            collective_id=collective_id, has_side_effects=True, vmem_limit_bytes=VMEM_LIMIT
        ),
    )(*operands)


def routing(route_ids, route_gates, pair, half):
    ids = lax.dynamic_index_in_dim(route_ids, pair, 0, keepdims=False)
    gates = lax.dynamic_index_in_dim(route_gates, pair, 0, keepdims=False)
    shares = gates / jnp.sum(gates, axis=-1, keepdims=True)
    ids, shares = (jnp.where(pair == 0, value, value[::-1]) for value in (ids, shares))
    uses, batches, tokens, top = ids.shape
    flat = ids.reshape(uses, batches, tokens * top)
    before = jnp.tri(tokens * top, k=-1, dtype=jnp.bool_)
    position = jnp.sum((flat[..., :, None] == flat[..., None, :]) & before, axis=-1)
    away = (flat - lax.axis_index("expert") + EXPERTS) % EXPERTS
    batch = jnp.arange(batches, dtype=jnp.int32)[None, :, None]
    slot = away * MSG + batch * (MSG // 2) + lax.axis_index("dp") * 2 + position % 2
    slot = jnp.where(position // 2 == half, slot, -1)
    both = jnp.stack([slot.astype(F32).reshape(ids.shape), shares], axis=-1)
    both = both.reshape(uses, batches * tokens, top, 2)
    both = lax.all_gather(both, "dp", axis=1, tiled=True)
    slots, shares = both[..., 0].astype(jnp.int32), both[..., 1]
    return slots, shares


def local(stream_in, cotangent, route_ids, route_gates, norm_gain, up_weight, down_weight):
    section = lax.axis_index("section")
    pair, half = section // 2, section % 2
    slots, shares = routing(route_ids, route_gates, pair, half)
    slot_rows, share_rows = slots.transpose(0, 2, 1), shares.transpose(0, 2, 1)
    gain = lax.dynamic_slice(norm_gain, (pair, lax.axis_index("dp") * PART), (1, PART))
    up, down = up_weight[0, 0], down_weight[0, 0]

    dma = pltpu.SemaphoreType.DMA
    hidden, features = ((SLOTS, 2 * HALF), BF16), ((SLOTS, PART), BF16)
    tokens, quarter = ((GROUPS, 2, 32, PART), BF16), ((CHUNKS, QUART, 2 * HALF), F32)
    handed_shape = ((2, TOKENS, PART), BF16)
    vm_hidden, vm_features = pltpu.VMEM(*hidden), pltpu.VMEM(*features)
    vm_landed = pltpu.VMEM((CHUNKS, 3, QUART, 2 * HALF), BF16)
    vm_leaving = pltpu.VMEM((TOKENS, PART), BF16)
    vm_token = [pltpu.VMEM((8, TOKENS), F32), pltpu.VMEM((3, 8, TOKENS), F32)]
    sem_group, sem_peers = dma((2, CHUNKS, 3)), dma((2, EXPERTS))

    rows1, pre1, act1, handed, cotan, up_other, down_other = call(
        first_forward,
        0,
        [features, quarter, hidden, handed_shape, tokens, ((PART, HALF), BF16), ((HALF, PART), BF16)],
        [pltpu.VMEM(*tokens), vm_features, vm_hidden, vm_landed, vm_features, vm_features, vm_leaving, *vm_token]
        + [dma((2, 4)), dma((2, 4)), dma((2, 2)), dma((2, 3)), sem_peers]
        + [sem_group, sem_group, sem_peers, dma((2, 2))],
        stream_in, cotangent, up, down, gain, slot_rows[0], slots[0], shares[0],
    )
    rows2, act2, grads2, pre_grad2, handed_back = call(
        second_layer,
        1,
        [features, hidden, features, hidden, handed_shape],
        [vm_features, vm_features, vm_hidden, vm_landed, vm_hidden, vm_landed, vm_features, vm_features, vm_leaving]
        + [*vm_token, *vm_token, dma((2, 3)), dma((2, 3)), sem_peers, sem_peers]
        + [sem_group, sem_group, sem_group, sem_group, sem_peers, dma((2, 2))],
        handed, cotan, up, up_other, down, down_other, gain, slot_rows[1], slots[1], share_rows[1],
    )
    grad_up, grad_down = call(
        first_backward,
        2,
        [((PART, HALF), BF16), ((HALF, PART), BF16)],
        [vm_features, vm_features, vm_hidden, vm_hidden, vm_landed]
        + [pltpu.VMEM((PART, 2 * HALF), F32), pltpu.VMEM((2 * HALF, PART), F32)]
        + [pltpu.VMEM((PART, HALF), BF16), pltpu.VMEM((HALF, PART), BF16)] * 2
        + [sem_peers, sem_group, sem_group, dma((2, 2))],
        handed_back, down, down_other, slot_rows[0], share_rows[0],
        rows1, act1, pre1, rows2, act2, grads2, pre_grad2,
    )
    return grad_up[None, None], grad_down[None, None]


def solution(mesh):
    placed = (
        P(None, None, ("expert", "dp"), "section"),
        P(None, None, ("expert", "dp"), "section"),
        P(None, None, None, ("expert", "dp"), None),
        P(None, None, None, ("expert", "dp"), None),
        P(),
        P("section", "expert", "dp", None),
        P("section", "expert", None, "dp"),
    )
    return jax.shard_map(
        local,
        mesh=mesh,
        in_specs=placed,
        out_specs=(P("section", "expert", "dp", None), P("section", "expert", None, "dp")),
        check_vma=False,
    )
```

time: 1490 us -> 511 us (0.34)
  the two profiles are of different devices: /device:TPU:6 before, /device:TPU:220 now
where the time goes in v1:
time: 511 us
  Pallas kernels  481 us (94%)
  blocking collectives  15.6 us (3%)
  local copies, waits for them, and re-layouts  13.4 us (3%)
    pallas_call x3, Pallas kernels, call(): pl.pallas_call(kernel, out_shape=[jax.ShapeDtypeStruct(shape, dtype) for...  481 us
    all_gather x1, blocking collectives, routing(): both = lax.all_gather(both, 'dp', axis=1, tiled=True)  15.6 us

profile of v1, /device:TPU:220, one launch (start us, length us, event | category | flops | bytes accessed | tf_op | source)
XLA Modules:
  0.0 510.9 jit_solution(6944532163240369744)
XLA Ops:
  0.9 0.5 copy-done.2
  1.4 1.4 dynamic_slice.11.gain
  2.9 0.1 copy.69
  3.1 0.1 copy.56
  3.2 0.1 eq.39
  3.3 0.2 convert_reduce_fusion
  3.5 0.1 reduce_sum.21
  3.7 0.1 fusion.7
  3.8 0.9 copy.63
  4.7 15.6 %all_gather.3 = f32[2,256,2,2]{3,2,0,1:T(2,128)S(1)} all-gather(f32[2,64,2,2]{3,2,0,1:T(2,128)S(1)} %copy.63), channel_id=1, replica_groups=mesh['section'=4,'expert'=32,'dp'=4] {'dp'}, dimensions={1}, use_global_device_ids=true | all-gather | bytes 10240 | tf_op jit(solution)/shard_map/all_gather | solution.py:590
  20.3 0.3 slice.44
  20.6 2.3 copy.74
  22.9 0.7 fusion.10
  23.6 0.3 copy.75
  23.9 0.6 slice_bitcast_fusion
  24.5 0.3 copy.73
  24.8 0.6 slice_bitcast_fusion.3
  25.4 0.8 copy.68.slot_col
  26.2 0.8 copy.66.slot_col
  27.0 167.1 %shard_map.86 = (bf16[512,896]{1,0:T(8,128)(2,1)}, f32[2,64,1024]{2,1,0:T(8,128)}, bf16[512,1024]{1,0:T(8,128)(2,1)}, bf16[2,256,896]{2,1,0:T(8,128)(2,1)}, bf16...) custom-call(bf16[2,2,32,896]{3,2,1,0:T(8,128)(2,1)} %stream.1, ...), custom_call_target="tpu_custom_call" | custom-call | tf_op jit(solution)/shard_map/pallas_call | solution.py:563
  194.1 185.6 %shard_map.87 = (bf16[512,896]{1,0:T(8,128)(2,1)}, bf16[512,1024]{1,0:T(8,128)(2,1)}, bf16[512,896]{1,0:T(8,128)(2,1)}, bf16[512,1024]{1,0:T(8,128)(2,1)}, bf16[2,256,896]{2,1,0:T(8,128)(2,1)}) custom-call(bf16[2,256,896]{2,1,0:T(8,128)(2,1)} %get-tuple-element.16.handed, bf16[4,2,32,896]{3,2,1,0:T(8,128)(2,1)} %get-tuple-element.17.cotan, ...), custom_call_target="tpu_custom_call" | custom-call | tf_op jit(solution)/shard_map/pallas_call | solution.py:563
  379.8 127.9 %shard_map.88 = (bf16[896,512]{1,0:T(8,128)(2,1)}, bf16[512,896]{1,0:T(8,128)(2,1)}) custom-call(bf16[2,256,896]{2,1,0:T(8,128)(2,1)} %get-tuple-element.20.handed_back, bf16[512,896]{1,0:T(8,128)(2,1)} %bitcast.37, bf16[512,896]{1,0:T(8,128)(2,1)} %get-tuple-element.19.down_other, s32[2,256]{1,0:T(2,128)} %get-tuple-element.39.slot_row, ...), custom_call_target="tpu_custom_call" | custom-call | tf_op jit(solution)/shard_map/pallas_call | solution.py:563
  507.7 2.2 copy.78
  510.0 0.9 copy.79
  (19 shorter events, 0.4 us)
Async XLA Ops:
  0.6 2.2 copy-start
  0.7 0.7 copy-start.2
  507.7 2.3 copy-start.1

commit v2 on v0

v2 whole, which is shorter than its diff:
```python
import jax
import jax.numpy as jnp
from jax import lax
from jax.experimental import pallas as pl
from jax.experimental.pallas import tpu as pltpu
from jax.sharding import PartitionSpec as P

EPSILON = 1e-06
MESH = pl.DeviceIdType.MESH
F32 = jnp.float32
BF16 = jnp.bfloat16
EXPERTS = 32
GROUPS = 4
BATCHES = 2
BLOCK = 32
TOKENS = GROUPS * BLOCK
MSG = 8
SLOTS = EXPERTS * MSG
QUART = SLOTS // GROUPS
PART = 896
HALF = 512
VMEM_LIMIT = 56 * 1024 * 1024


def dot(a, b):
    return lax.dot_general(a, b, (((1,), (0,)), ((), ())), preferred_element_type=F32)


def dot_t(a, b):
    return lax.dot_general(a, b, (((1,), (1,)), ((), ())), preferred_element_type=F32)


def t_dot(a, b):
    return lax.dot_general(a, b, (((0,), (0,)), ((), ())), preferred_element_type=F32)


def copy_to(src, dst, send_sem, recv_sem, device):
    return pltpu.make_async_remote_copy(
        src_ref=src,
        dst_ref=dst,
        send_sem=send_sem,
        recv_sem=recv_sem,
        device_id=device,
        device_id_type=MESH,
    )


class Place:
    def __init__(self):
        self.section = lax.axis_index("section")
        self.expert = lax.axis_index("expert")
        self.group = lax.axis_index("dp")
        self.half = self.section % 2
        self.pair = self.section // 2
        self.partner = self.section + 1 - 2 * self.half


def greet_experts(here, barrier):
    def one(k, carry):
        pl.semaphore_signal(
            barrier,
            inc=1,
            device_id={"expert": (here.expert + k) % EXPERTS},
            device_id_type=MESH,
        )
        return carry

    lax.fori_loop(1, EXPERTS, one, 0)


def greet(barrier, device):
    pl.semaphore_signal(barrier, inc=1, device_id=device, device_id_type=MESH)


class Exchange:
    def __init__(self, here, src, dst, sems, sign):
        self.here, self.src, self.dst, self.sems, self.sign = here, src, dst, sems, sign

    def copy(self, k, count=1):
        which = pl.ds(k, count)
        peer = (self.here.expert + self.sign * k + EXPERTS) % EXPERTS
        return copy_to(
            self.src.at[which], self.dst.at[which], self.sems.at[0], self.sems.at[1], {"expert": peer}
        )

    def start(self, rows):
        messages = rows.reshape(EXPERTS, MSG, PART).astype(BF16)
        self.src[...] = messages
        self.dst[0:1] = messages[0:1]

        def one(k, carry):
            self.copy(k).start()
            return carry

        lax.fori_loop(1, EXPERTS, one, 0)

    def take(self):
        self.copy(1, EXPERTS - 1).wait_recv()
        return self.dst[...].astype(F32).reshape(SLOTS, PART).astype(BF16)

    def wait_send(self):
        self.copy(1, EXPERTS - 1).wait_send()


class GroupSum:
    def __init__(self, here, parts, landed, sems):
        self.here, self.parts, self.landed, self.sems = here, parts, landed, sems

    def copy(self, j):
        peer = (self.here.group + j) % GROUPS
        rows = pl.ds(pl.multiple_of(peer * QUART, QUART), QUART)
        return copy_to(
            self.parts.at[rows],
            self.landed.at[j - 1],
            self.sems.at[0, j - 1],
            self.sems.at[1, j - 1],
            {"dp": peer},
        )

    def start(self, near, far):
        self.parts[:, 0:HALF] = near.astype(BF16)
        self.parts[:, HALF:] = far.astype(BF16)
        for j in (2, 1, 3):
            self.copy(j).start()

    def total(self):
        for j in (1, 3, 2):
            self.copy(j).wait_recv()
        rows = pl.ds(pl.multiple_of(self.here.group * QUART, QUART), QUART)
        value = self.parts[rows].astype(F32)
        for j in (1, 2, 3):
            value = value + self.landed[j - 1].astype(F32)
        return value

    def wait_send(self):
        for j in (1, 2, 3):
            self.copy(j).wait_send()


class GroupGather:
    def __init__(self, here, whole, sems):
        self.here, self.whole, self.sems = here, whole, sems

    def rows(self, back):
        quarter = (self.here.group + GROUPS - back) % GROUPS
        return pl.ds(pl.multiple_of(quarter * QUART, QUART), QUART)

    def copy(self, to, back, half, slot):
        where = self.whole.at[self.rows(back), pl.ds(half * HALF, HALF)]
        return copy_to(
            where, where, self.sems.at[0, slot], self.sems.at[1, slot],
            {"dp": (self.here.group + to) % GROUPS},
        )

    def start(self, value):
        self.whole[self.rows(0)] = value
        for slot, (to, half) in enumerate(((1, 0), (3, 1), (1, 1), (3, 0))):
            self.copy(to, 0, half, slot).start()

    def pass_on(self):
        self.copy(1, 1, 0, 0).wait_recv()
        self.copy(1, 1, 0, 4).start()
        self.copy(3, 3, 1, 1).wait_recv()
        self.copy(3, 3, 1, 5).start()

    def wait_recv(self):
        self.copy(1, 1, 1, 2).wait_recv()
        self.copy(3, 3, 0, 3).wait_recv()
        self.copy(1, 2, 0, 4).wait_recv()
        self.copy(3, 2, 1, 5).wait_recv()

    def wait_send(self):
        for slot, (to, half) in enumerate(((1, 0), (3, 1), (1, 1), (3, 0))):
            self.copy(to, 0, half, slot).wait_send()
        self.copy(1, 1, 0, 4).wait_send()
        self.copy(3, 3, 1, 5).wait_send()


class SmallSum:
    def __init__(self, here, own, landed, sems):
        self.here, self.own, self.landed, self.sems = here, own, landed, sems

    def copy(self, j):
        return copy_to(
            self.own,
            self.landed.at[j - 1],
            self.sems.at[0, j - 1],
            self.sems.at[1, j - 1],
            {"dp": (self.here.group + j) % GROUPS},
        )

    def start(self):
        for j in (2, 1, 3):
            self.copy(j).start()

    def start_column(self, column):
        self.own[...] = jnp.broadcast_to(column, (TOKENS, TOKENS)).T[0:8]
        self.start()

    def total(self):
        for j in (1, 3, 2):
            self.copy(j).wait_recv()
        return self.own[...] + self.landed[0] + self.landed[1] + self.landed[2]

    def total_column(self):
        return jnp.broadcast_to(self.total()[0:1], (TOKENS, TOKENS)).T[:, 0:1]

    def wait_send(self):
        for j in (1, 2, 3):
            self.copy(j).wait_send()


class HandOn:
    def __init__(self, here, leaving, handed, sems):
        self.here, self.leaving, self.handed, self.sems = here, leaving, handed, sems

    def copy(self, to, owner):
        return copy_to(
            self.leaving, self.handed.at[owner], self.sems.at[0, to], self.sems.at[1, owner],
            {"section": 2 * (1 - self.here.pair) + to},
        )

    def start(self, value):
        self.leaving[...] = value.astype(BF16)
        for to in range(2):
            self.copy(to, self.here.half).start()

    def take(self):
        for owner in range(2):
            self.copy(0, owner).wait_recv()
        return (self.handed[0].astype(F32) + self.handed[1].astype(F32)).astype(BF16)

    def again(self):
        return (self.handed[0].astype(F32) + self.handed[1].astype(F32)).astype(BF16)

    def wait_send(self):
        for to in range(2):
            self.copy(to, self.here.half).wait_send()


class Cut:
    def __init__(self, here, source, target, sems, flip):
        self.here, self.source, self.target, self.sems, self.flip = here, source, target, sems, flip

    def copy(self, m, section, owner):
        direction = 1 - section // 2 if self.flip else section // 2
        return copy_to(
            self.source.at[direction, m], self.target.at[m, owner],
            self.sems.at[0, m, section], self.sems.at[1, m, owner],
            {"section": section, "dp": self.here.section},
        )

    def start(self, m):
        for section in range(4):
            direction = 1 - section // 2 if self.flip else section // 2
            stays = (self.here.section == section) & (self.here.group == section)

            @pl.when(stays)
            def _():
                self.target[m, pl.ds(self.here.group, 1)] = self.source[direction, m : m + 1]

            @pl.when(jnp.logical_not(stays))
            def _():
                self.copy(m, section, self.here.group).start()

    def take(self, m):
        for owner in range(4):
            stays = (self.here.section == self.here.group) & (self.here.group == owner)

            @pl.when(jnp.logical_not(stays))
            def _():
                self.copy(m, 0, owner).wait_recv()

    def value(self, m):
        return self.target[m].reshape(TOKENS, PART)

    def wait_send(self):
        for m in range(BATCHES):
            for section in range(4):
                stays = (self.here.section == section) & (self.here.group == section)

                @pl.when(jnp.logical_not(stays))
                def _():
                    self.copy(m, section, self.here.group).wait_send()


class Routes:
    def __init__(self, rows, columns):
        self.rows, self.columns = rows, columns

    def by_slot(self, u, m):
        slots = lax.broadcasted_iota(jnp.int32, (SLOTS, TOKENS), 0).astype(F32)
        at = m * 8 + u * 4
        return [(slots == self.rows[at + 2 * k : at + 2 * k + 1], self.rows[at + 2 * k + 1 : at + 2 * k + 2]) for k in range(2)]

    def by_token(self, u, m):
        slots = lax.broadcasted_iota(jnp.int32, (TOKENS, SLOTS), 1).astype(F32)
        at = m * 8 + u * 4
        return [(slots == self.columns[:, at + 2 * k : at + 2 * k + 1], self.columns[:, at + 2 * k + 1 : at + 2 * k + 2]) for k in range(2)]


def marks(picks):
    (first, _), (second, _) = picks
    return jnp.where(first | second, 1.0, 0.0).astype(BF16)


def weighted(picks):
    (first, share), (second, other) = picks
    return jnp.where(first, share, 0.0) + jnp.where(second, other, 0.0)


def exact_dot(weights, values):
    high = weights.astype(BF16)
    low = (weights - high.astype(F32)).astype(BF16)
    return dot(high, values) + dot(low, values)


def norm_scale(total):
    return lax.rsqrt(total * (1.0 / (GROUPS * PART)) + EPSILON)


def silu(pre):
    return pre * jax.nn.sigmoid(pre)


def pre_gradient(act_grad, pre):
    gate = jax.nn.sigmoid(pre)
    return (act_grad * gate * (1.0 + pre * (1.0 - gate))).astype(BF16)


def row_sum(values):
    return jnp.sum(values, axis=1, keepdims=True)


def update(
    stream, cotangent, up, down, norm_gain, routes_own,
    grad_up, grad_down,
    layer_in, cotan, up_other, down_other, routes_landed, routes_rows, routes_columns,
    sent, came, rows1, rows2, grads1, grads2, parts, landed, gathered, pre1, pre2,
    small_own, small_landed, scales, leaving, handed,
    sum_up, sum_down, give_up, give_down, got_up, got_down,
    cut_sems, pair_sems, route_sems, small_sems, peer_sems, sum_sems, gather_sems, hand_sems,
):
    here = Place()
    both = range(BATCHES)
    barrier = pltpu.get_barrier_semaphore()
    greet_experts(here, barrier)

    def greet_other(i, carry):
        at = (here.section * GROUPS + here.group + i) % 16
        greet(barrier, {"section": at // GROUPS, "dp": at % GROUPS})
        return carry

    lax.fori_loop(1, 16, greet_other, 0)
    pl.semaphore_wait(barrier, EXPERTS - 1 + 15)

    def exchanges(i, sign):
        return [Exchange(here, sent.at[i, m], came.at[i, m], peer_sems.at[i, m], sign) for m in both]

    go1, back1, go_grads, go2, back2, go3 = (
        exchanges(i, sign) for i, sign in enumerate((1, -1, 1, 1, -1, 1))
    )
    sum1, sum2, sum_grads2, sum_grads1 = (
        [GroupSum(here, parts.at[i, m], landed.at[i, m], sum_sems.at[i, m]) for m in both] for i in range(4)
    )
    act1, act2, pre_grad2, pre_grad1 = ([gathered.at[i, m] for m in both] for i in range(4))
    all_act1, all_act2, all_pre_grad2, all_pre_grad1 = (
        [GroupGather(here, gathered.at[i, m], gather_sems.at[i, m]) for m in both] for i in range(4)
    )
    norm1, norm2, mix = (
        [SmallSum(here, small_own.at[i, m], small_landed.at[i, m], small_sems.at[i, m]) for m in both]
        for i in range(3)
    )
    hand1, hand2 = (
        [HandOn(here, leaving.at[i, m], handed.at[i, m], hand_sems.at[i, m]) for m in both] for i in range(2)
    )
    cut_in = Cut(here, stream, layer_in, cut_sems.at[0], False)
    cut_cotan = Cut(here, cotangent, cotan, cut_sems.at[1], True)
    route_sum = SmallSum(here, routes_own, routes_landed, route_sems)
    routes = Routes(routes_rows, routes_columns)
    to_partner = {"section": here.partner}

    def pair_copy(i, source, target):
        return copy_to(source, target, pair_sems.at[0, i], pair_sems.at[1, i], to_partner)

    up_copy, down_copy = pair_copy(0, up, up_other), pair_copy(1, down, down_other)
    give_down_copy, give_up_copy = pair_copy(2, give_down, got_down), pair_copy(3, give_up, got_up)
    gain = norm_gain[pl.ds(here.pair, 1), pl.ds(pl.multiple_of(here.group * PART, PART), PART)]
    first_half = (1 - here.half).astype(F32)

    def up_parts(rows, target):
        target.start(dot(rows[...], up[...]), dot(rows[...], up_other[...]))

    def down_parts(rows, target):
        target.start(dot_t(rows[...], down[...]), dot_t(rows[...], down_other[...]))

    route_sum.start()
    for m in both:
        cut_in.start(m)
    up_copy.start()
    for m in both:
        cut_in.take(m)
        values = cut_in.value(m).astype(F32)
        norm1[m].start_column(row_sum(values * values))
    total = route_sum.total()
    routes_rows[...] = total
    routes_columns[...] = jnp.concatenate([total] * (TOKENS // total.shape[0]), axis=0).T
    for m in both:
        scale = norm_scale(norm1[m].total_column())
        normed = (cut_in.value(m).astype(F32) * scale * gain).astype(BF16)
        go1[m].start(dot(marks(routes.by_slot(0, m)), normed))
    down_copy.start()
    for m in both:
        cut_cotan.start(m)
    up_copy.wait_recv()
    for m in both:
        rows1[m] = go1[m].take()
        up_parts(rows1.at[m], sum1[m])
    for m in both:
        cut_cotan.take(m)
        go_grads[m].start(exact_dot(weighted(routes.by_slot(1, m)), cut_cotan.value(m)))
    for m in both:
        pre1[m] = sum1[m].total()
        all_act1[m].start(silu(pre1[m]).astype(BF16))
    for m in both:
        all_act1[m].pass_on()
    down_copy.wait_recv()
    for m in both:
        all_act1[m].wait_recv()
        act = act1[m]
        back1[m].start(dot(act[:, 0:HALF], down[...]) + dot(act[:, HALF:], down_other[...]))
    for m in both:
        grads2[m] = go_grads[m].take()
        down_parts(grads2.at[m], sum_grads2[m])
    for m in both:
        expert_out = back1[m].take()
        direct = cut_in.value(m).astype(F32) * first_half
        hand1[m].start(direct + exact_dot(weighted(routes.by_token(0, m)), expert_out))

    for m in both:
        values = hand1[m].take().astype(F32)
        norm2[m].start_column(row_sum(values * values))
        scales[m] = norm_scale(norm2[m].total_column())
        normed = (hand1[m].again().astype(F32) * scales[m] * gain).astype(BF16)
        go2[m].start(dot(marks(routes.by_slot(1, m)), normed))
    for m in both:
        rows2[m] = go2[m].take()
        up_parts(rows2.at[m], sum2[m])
    for m in both:
        pre2[m] = sum2[m].total()
        all_pre_grad2[m].start(pre_gradient(sum_grads2[m].total(), pre2[m]))
    for m in both:
        all_pre_grad2[m].pass_on()
    for m in both:
        all_pre_grad2[m].wait_recv()
        grad = pre_grad2[m]
        back2[m].start(dot_t(grad[:, 0:HALF], up[...]) + dot_t(grad[:, HALF:], up_other[...]))
    for m in both:
        all_act2[m].start(silu(pre2[m]).astype(BF16))

    @pl.loop(0, PART // 128)
    def _(i):
        at = pl.ds(pl.multiple_of(i * 128, 128), 128)
        sum_up[at] = t_dot(rows2[0, :, at], pre_grad2[0][...]) + t_dot(rows2[1, :, at], pre_grad2[1][...])

    for m in both:
        scaled = dot(marks(routes.by_token(1, m)), back2[m].take()) * gain
        mix[m].start_column(row_sum(hand1[m].again().astype(F32) * scaled))
        direct = cut_cotan.value(m).astype(F32) * first_half + scales[m] * scaled
        mean = mix[m].total_column() * (1.0 / (GROUPS * PART))
        scale = scales[m]
        hand2[m].start(direct - hand1[m].again().astype(F32) * (scale * scale * scale * mean))
    for m in both:
        all_act2[m].pass_on()
    for m in both:
        all_act2[m].wait_recv()

    @pl.loop(0, 2 * HALF // 128)
    def _(i):
        at = pl.ds(pl.multiple_of(i * 128, 128), 128)
        sum_down[at] = t_dot(act2[0][:, at], grads2[0]) + t_dot(act2[1][:, at], grads2[1])

    for m in both:
        incoming = hand2[m].take()
        go3[m].start(exact_dot(weighted(routes.by_slot(0, m)), incoming))
    for m in both:
        grads1[m] = go3[m].take()
        down_parts(grads1.at[m], sum_grads1[m])

    @pl.loop(0, HALF // 128)
    def _(i):
        at = pl.ds(pl.multiple_of(i * 128, 128), 128)
        far = pl.ds(pl.multiple_of(HALF + i * 128, 128), 128)
        value = sum_down[far] + t_dot(act1[0][:, far], grads1[0]) + t_dot(act1[1][:, far], grads1[1])
        give_down[at] = value.astype(BF16)

    give_down_copy.start()
    for m in both:
        all_pre_grad1[m].start(pre_gradient(sum_grads1[m].total(), pre1[m]))
    for m in both:
        all_pre_grad1[m].pass_on()

    @pl.loop(0, HALF // 128)
    def _(i):
        at = pl.ds(pl.multiple_of(i * 128, 128), 128)
        sum_down[at] += t_dot(act1[0][:, at], grads1[0]) + t_dot(act1[1][:, at], grads1[1])

    for m in both:
        all_pre_grad1[m].wait_recv()

    @pl.loop(0, PART // 128)
    def _(i):
        at = pl.ds(pl.multiple_of(i * 128, 128), 128)
        value = sum_up[at, HALF:]
        for m in both:
            value = value + t_dot(rows1[m, :, at], pre_grad1[m][:, HALF:])
        give_up[at] = value.astype(BF16)

    give_up_copy.start()

    @pl.loop(0, PART // 128)
    def _(i):
        at = pl.ds(pl.multiple_of(i * 128, 128), 128)
        for m in both:
            sum_up[at, 0:HALF] += t_dot(rows1[m, :, at], pre_grad1[m][:, 0:HALF])

    give_down_copy.wait_recv()
    grad_down[...] = (sum_down[0:HALF] + got_down[...].astype(F32)).astype(BF16)
    give_up_copy.wait_recv()
    grad_up[...] = (sum_up[:, 0:HALF] + got_up[...].astype(F32)).astype(BF16)

    for sender in (cut_in, cut_cotan, route_sum, up_copy, down_copy, give_down_copy, give_up_copy):
        sender.wait_send()
    for senders in (go1, back1, go_grads, go2, back2, go3, sum1, sum2, sum_grads2, sum_grads1, all_act1,
                    all_act2, all_pre_grad2, all_pre_grad1, norm1, norm2, mix, hand1, hand2):
        for m in both:
            senders[m].wait_send()


def routing(route_ids, route_gates, pair, half):
    ids = lax.dynamic_index_in_dim(route_ids, pair, 0, keepdims=False)
    gates = lax.dynamic_index_in_dim(route_gates, pair, 0, keepdims=False)
    shares = gates / jnp.sum(gates, axis=-1, keepdims=True)
    ids, shares = (jnp.where(pair == 0, value, value[::-1]) for value in (ids, shares))
    uses, batches, tokens, top = ids.shape
    flat = ids.reshape(uses, batches, tokens * top)
    before = jnp.tri(tokens * top, k=-1, dtype=jnp.bool_)
    position = jnp.sum((flat[..., :, None] == flat[..., None, :]) & before, axis=-1)
    away = (flat - lax.axis_index("expert") + EXPERTS) % EXPERTS
    group = lax.axis_index("dp")
    slot = away * MSG + group * 2 + position % 2
    slot = jnp.where(position // 2 == half, slot, -1).astype(F32).reshape(ids.shape)
    values = jnp.stack([slot, shares], axis=-1).transpose(1, 0, 3, 4, 2).reshape(batches * uses * top * 2, tokens)
    lanes = jnp.arange(TOKENS, dtype=jnp.int32)[None, :] // BLOCK
    return jnp.where(lanes == group, jnp.tile(values, (1, GROUPS)), 0.0)


def local(stream_in, cotangent, route_ids, route_gates, norm_gain, up_weight, down_weight):
    section = lax.axis_index("section")
    routes = routing(route_ids, route_gates, section // 2, section % 2)
    dma, vmem = pltpu.SemaphoreType.DMA, pltpu.VMEM
    whole = pl.BlockSpec(memory_space=pltpu.VMEM)
    messages = vmem((6, BATCHES, EXPERTS, MSG, PART), BF16)
    features = vmem((BATCHES, SLOTS, PART), BF16)
    hidden = vmem((4, BATCHES, SLOTS, 2 * HALF), BF16)
    quarters = vmem((BATCHES, QUART, 2 * HALF), F32)
    cut = vmem((BATCHES, GROUPS, BLOCK, PART), BF16)
    up_half, down_half = vmem((PART, HALF), BF16), vmem((HALF, PART), BF16)
    scratch = [
        cut, cut, up_half, down_half,
        vmem((3, 16, TOKENS), F32), vmem((16, TOKENS), F32), vmem((TOKENS, TOKENS), F32),
        messages, messages, features, features, features, features,
        hidden, vmem((4, BATCHES, 3, QUART, 2 * HALF), BF16), hidden, quarters, quarters,
        vmem((3, BATCHES, 8, TOKENS), F32), vmem((3, BATCHES, 3, 8, TOKENS), F32), vmem((BATCHES, TOKENS, 1), F32),
        vmem((2, BATCHES, TOKENS, PART), BF16), vmem((2, BATCHES, 2, TOKENS, PART), BF16),
        vmem((PART, 2 * HALF), F32), vmem((2 * HALF, PART), F32),
        up_half, down_half, up_half, down_half,
        dma((2, 2, BATCHES, 4)), dma((2, 4)), dma((2, 3)), dma((3, BATCHES, 2, 3)), dma((6, BATCHES, 2)),
        dma((4, BATCHES, 2, 3)), dma((4, BATCHES, 2, 6)), dma((2, BATCHES, 2, 2)),
    ]
    grad_up, grad_down = pl.pallas_call(
        update,
        out_shape=[jax.ShapeDtypeStruct((PART, HALF), BF16), jax.ShapeDtypeStruct((HALF, PART), BF16)],
        in_specs=[whole] * 6,
        out_specs=[whole] * 2,
        scratch_shapes=scratch,
        compiler_params=pltpu.CompilerParams(
            collective_id=0, has_side_effects=True, vmem_limit_bytes=VMEM_LIMIT
        ),
    )(stream_in, cotangent, up_weight[0, 0], down_weight[0, 0], norm_gain, routes)
    return grad_up[None, None], grad_down[None, None]


def solution(mesh):
    placed = (
        P(None, None, ("expert", "dp"), "section"),
        P(None, None, ("expert", "dp"), "section"),
        P(None, None, None, ("expert", "dp"), None),
        P(None, None, None, ("expert", "dp"), None),
        P(),
        P("section", "expert", "dp", None),
        P("section", "expert", None, "dp"),
    )
    return jax.shard_map(
        local,
        mesh=mesh,
        in_specs=placed,
        out_specs=(P("section", "expert", "dp", None), P("section", "expert", None, "dp")),
        check_vma=False,
    )
```

time: 1490 us -> 369 us (0.25)
  waiting for transfers between devices: 795 us -> 0 us
  Pallas kernels: 0 us -> 360 us
  blocking collectives: 321 us -> 0 us
  starting transfers between devices: 182 us -> 0 us
  matrix products: 57.7 us -> 0 us
  local copies, waits for them, and re-layouts: 59.6 us -> 4.55 us
  other arithmetic: 54.6 us -> 1.19 us
    psum x8 -> x0, waiting for transfers between devices: 432 us -> none  [hidden_total(): lax.psum(partial_value.astype(jnp.bfloat16), 'dp').astype(jnp.float32)]
    pallas_call x0 -> x1, Pallas kernels: none -> 360 us  [local(): pl.pallas_call(update, out_shape=[jax.ShapeDtypeStruct((PART, HALF), BF16...]
    all_to_all x8 -> x0, blocking collectives: 284 us -> none  [swap_rows(): lax.all_to_all(flat_rows, ('expert', 'dp'), split_axis=0, concat_axis=0,...]
    all_to_all x8 -> x0, waiting for transfers between devices: 189 us -> none  [swap_rows(): lax.all_to_all(flat_rows, ('expert', 'dp'), split_axis=0, concat_axis=0,...]
    ppermute x24 -> x0, waiting for transfers between devices: 174 us -> none  [the longest x8 159 us: swapped(): lax.ppermute(x, axis, [(i, i ^ 1 << distance) for i in range(lax.axis_siz...]
    all_to_all x8 -> x0, starting transfers between devices: 98 us -> none  [swap_rows(): lax.all_to_all(flat_rows, ('expert', 'dp'), split_axis=0, concat_axis=0,...]
    ppermute x24 -> x0, starting transfers between devices: 83.8 us -> none  [the longest x16 61.7 us: passed_along(): return lax.ppermute(block, axis, route)]
    dot_general x34 -> x0, matrix products: 57.7 us -> none  [the longest x4 10.9 us: backward_turn(): lax.dot_general(grad_recv, w_down, contract_last, preferred_element_type=...]
  transfers between devices with their start and end apart: 40 -> 0, of which waited for: 36 -> 0; matrix products, arithmetic and copies ran while one was open for 3% -> 0% of each run, Pallas kernels for 0% -> 0%
where the time goes in v2:
time: 369 us; the launch traced here: 367 us
  Pallas kernels  360 us (98%)
  local copies, waits for them, and re-layouts  4.55 us (1%)
    pallas_call x1, Pallas kernels, local(): pl.pallas_call(update, out_shape=[jax.ShapeDtypeStruct((PART, HALF), BF16...  360 us

profile of v2, /device:TPU:6, one launch (start us, length us, event | category | flops | bytes accessed | tf_op | source)
XLA Modules:
  0.0 366.7 jit_solution(1959415964118706975)
XLA Ops:
  0.6 0.0 copy-start
  0.7 0.0 copy-start.2
  0.7 0.6 copy-done
  1.3 0.0 copy-done.2
  1.4 0.1 iota_compare_fusion
  1.5 0.1 copy.17
  1.6 0.1 eq.46
  1.7 0.2 convert_reduce_fusion
  1.9 0.1 reduce_sum.21
  2.1 0.1 fusion.7
  2.2 0.1 copy.19
  2.3 0.1 copy.18
  2.4 0.1 bitcast_divide_fusion
  2.5 0.1 copy.20
  2.6 0.1 tile.12
  2.7 0.6 broadcast_select_fusion.routes_own
  3.3 360.2 %shard_map.86 = (bf16[896,512]{1,0:T(8,128)(2,1)}, bf16[512,896]{1,0:T(8,128)(2,1)}) custom-call(bf16[2,2,32,896]{3,2,1,0:T(8,128)(2,1)} %stream.1, bf16[2,2,32,896]{3,2,1,0:T(8,128)(2,1)} %cotangent.1, bf16[896,512]{1,0:T(8,128)(2,1)} %bitcast.16, bf16[512,896]{1,0:T(8,128)(2,1)} %bitcast.17, f32[2,3584]{1,0:T(2,128)} %norm_gain.1, ...), custom_call_target="tpu_custom_call" | custom-call | tf_op jit(solution)/shard_map/pallas_call | solution.py:581
  363.5 0.0 copy-start.1
  363.5 2.2 copy.24
  365.8 0.0 copy-done.1
  365.8 0.9 copy.25
  (9 shorter events, 0.1 us)
Async XLA Ops:
  0.6 0.7 copy-start
  0.7 0.7 copy-start.2
  363.5 2.3 copy-start.1

commit v3 on v2

--- a/solution.py
+++ b/solution.py
@@ -106,35 +106,43 @@
     def __init__(self, here, parts, landed, sems):
         self.here, self.parts, self.landed, self.sems = here, parts, landed, sems
 
-    def copy(self, j):
-        peer = (self.here.group + j) % GROUPS
-        rows = pl.ds(pl.multiple_of(peer * QUART, QUART), QUART)
+    def part(self, away, half):
+        quarter = (self.here.group + away) % GROUPS
+        rows = pl.ds(pl.multiple_of(quarter * QUART, QUART), QUART)
+        return self.parts.at[rows, pl.ds(half * HALF, HALF)]
+
+    def copy(self, slot):
+        away, half, to = ((2, 0, 1), (2, 1, 3), (1, 1, 1), (3, 0, 3), (1, 0, 1), (3, 1, 3))[slot]
         return copy_to(
-            self.parts.at[rows],
-            self.landed.at[j - 1],
-            self.sems.at[0, j - 1],
-            self.sems.at[1, j - 1],
-            {"dp": peer},
+            self.part(away, half), self.landed.at[slot], self.sems.at[0, slot], self.sems.at[1, slot],
+            {"dp": (self.here.group + to) % GROUPS},
         )
 
     def start(self, near, far):
         self.parts[:, 0:HALF] = near.astype(BF16)
         self.parts[:, HALF:] = far.astype(BF16)
-        for j in (2, 1, 3):
-            self.copy(j).start()
+        for slot in range(4):
+            self.copy(slot).start()
+
+    def pass_on(self):
+        for slot, away in ((0, 1), (1, 3)):
+            self.copy(slot).wait_recv()
+            part = self.part(away, slot)
+            part[...] = (part[...].astype(F32) + self.landed[slot].astype(F32)).astype(BF16)
+            self.copy(slot + 4).start()
 
     def total(self):
-        for j in (1, 3, 2):
-            self.copy(j).wait_recv()
-        rows = pl.ds(pl.multiple_of(self.here.group * QUART, QUART), QUART)
-        value = self.parts[rows].astype(F32)
-        for j in (1, 2, 3):
-            value = value + self.landed[j - 1].astype(F32)
-        return value
+        for slot in range(2, 6):
+            self.copy(slot).wait_recv()
+
+        def half(i, one, other):
+            return self.part(0, i)[...].astype(F32) + self.landed[one].astype(F32) + self.landed[other].astype(F32)
+
+        return jnp.concatenate([half(0, 3, 4), half(1, 2, 5)], axis=1)
 
     def wait_send(self):
-        for j in (1, 2, 3):
-            self.copy(j).wait_send()
+        for slot in range(6):
+            self.copy(slot).wait_send()
 
 
 class GroupGather:
@@ -156,6 +164,15 @@
         self.whole[self.rows(0)] = value
         for slot, (to, half) in enumerate(((1, 0), (3, 1), (1, 1), (3, 0))):
             self.copy(to, 0, half, slot).start()
+
+    def start_near(self, value):
+        self.whole[self.rows(0), 0:HALF] = value
+        self.copy(1, 0, 0, 0).start()
+        self.copy(3, 0, 0, 3).start()
+
+    def start_far(self):
+        self.copy(3, 0, 1, 1).start()
+        self.copy(1, 0, 1, 2).start()
 
     def pass_on(self):
         self.copy(1, 1, 0, 0).wait_recv()
@@ -239,49 +256,53 @@
 
 
 class Cut:
-    def __init__(self, here, source, target, sems, flip):
-        self.here, self.source, self.target, self.sems, self.flip = here, source, target, sems, flip
-
-    def copy(self, m, section, owner):
-        direction = 1 - section // 2 if self.flip else section // 2
+    def __init__(self, here, source, middle, target, sems, flip):
+        self.here, self.source, self.middle, self.target = here, source, middle, target
+        self.sems, self.flip = sems, flip
+
+    def rows(self, m, section):
+        pair = section // 2
+        return self.source.at[1 - pair if self.flip else pair, m]
+
+    def across(self, m, j, owner):
+        to = (self.here.section + j) % 4
         return copy_to(
-            self.source.at[direction, m], self.target.at[m, owner],
-            self.sems.at[0, m, section], self.sems.at[1, m, owner],
-            {"section": section, "dp": self.here.section},
+            self.rows(m, to), self.middle.at[m, owner],
+            self.sems.at[0, 0, m, j - 1], self.sems.at[0, 1, m, j - 1], {"section": to},
+        )
+
+    def within(self, m, j, owner):
+        to = (self.here.group + j) % GROUPS
+        return copy_to(
+            self.middle.at[m, to], self.target.at[m, owner],
+            self.sems.at[1, 0, m, j - 1], self.sems.at[1, 1, m, j - 1], {"dp": to},
         )
 
     def start(self, m):
-        for section in range(4):
-            direction = 1 - section // 2 if self.flip else section // 2
-            stays = (self.here.section == section) & (self.here.group == section)
-
-            @pl.when(stays)
-            def _():
-                self.target[m, pl.ds(self.here.group, 1)] = self.source[direction, m : m + 1]
-
-            @pl.when(jnp.logical_not(stays))
-            def _():
-                self.copy(m, section, self.here.group).start()
+        for j in (2, 1, 3):
+            self.across(m, j, self.here.section).start()
+        self.middle[m, pl.ds(self.here.section, 1)] = self.rows(m, self.here.section)[...][None]
+
+    def pass_on(self, m):
+        for j in (1, 3, 2):
+            self.across(m, j, (self.here.section + 4 - j) % 4).wait_recv()
+        for j in (2, 1, 3):
+            self.within(m, j, self.here.group).start()
+        own = pl.ds(self.here.group, 1)
+        self.target[m, own] = self.middle[m, own]
 
     def take(self, m):
-        for owner in range(4):
-            stays = (self.here.section == self.here.group) & (self.here.group == owner)
-
-            @pl.when(jnp.logical_not(stays))
-            def _():
-                self.copy(m, 0, owner).wait_recv()
+        for j in (1, 3, 2):
+            self.within(m, j, (self.here.group + GROUPS - j) % GROUPS).wait_recv()
 
     def value(self, m):
         return self.target[m].reshape(TOKENS, PART)
 
     def wait_send(self):
         for m in range(BATCHES):
-            for section in range(4):
-                stays = (self.here.section == section) & (self.here.group == section)
-
-                @pl.when(jnp.logical_not(stays))
-                def _():
-                    self.copy(m, section, self.here.group).wait_send()
+            for j in (1, 2, 3):
+                self.across(m, j, self.here.section).wait_send()
+                self.within(m, j, self.here.group).wait_send()
 
 
 class Routes:
@@ -335,11 +356,11 @@
 def update(
     stream, cotangent, up, down, norm_gain, routes_own,
     grad_up, grad_down,
-    layer_in, cotan, up_other, down_other, routes_landed, routes_rows, routes_columns,
-    sent, came, rows1, rows2, grads1, grads2, parts, landed, gathered, pre1, pre2,
+    middle_in, middle_cotan, layer_in, cotan, up_other, down_other, routes_landed, routes_rows, routes_columns,
+    sent, came, rows1, rows1_other, rows2, grads1, grads2, parts, landed, gathered, pre1, pre2,
     small_own, small_landed, scales, leaving, handed,
-    sum_up, sum_down, give_up, give_down, got_up, got_down,
-    cut_sems, pair_sems, route_sems, small_sems, peer_sems, sum_sems, gather_sems, hand_sems,
+    sum_up, sum_down, give_up, give_down, got_up, got_down, far_quarter,
+    cut_sems, pair_sems, far_sems, route_sems, small_sems, peer_sems, sum_sems, gather_sems, hand_sems,
 ):
     here = Place()
     both = range(BATCHES)
@@ -374,8 +395,8 @@
     hand1, hand2 = (
         [HandOn(here, leaving.at[i, m], handed.at[i, m], hand_sems.at[i, m]) for m in both] for i in range(2)
     )
-    cut_in = Cut(here, stream, layer_in, cut_sems.at[0], False)
-    cut_cotan = Cut(here, cotangent, cotan, cut_sems.at[1], True)
+    cut_in = Cut(here, stream, middle_in, layer_in, cut_sems.at[0], False)
+    cut_cotan = Cut(here, cotangent, middle_cotan, cotan, cut_sems.at[1], True)
     route_sum = SmallSum(here, routes_own, routes_landed, route_sems)
     routes = Routes(routes_rows, routes_columns)
     to_partner = {"section": here.partner}
@@ -385,6 +406,15 @@
 
     up_copy, down_copy = pair_copy(0, up, up_other), pair_copy(1, down, down_other)
     give_down_copy, give_up_copy = pair_copy(2, give_down, got_down), pair_copy(3, give_up, got_up)
+    rows_copy = pair_copy(4, rows1, rows1_other)
+    own_quarter = pl.ds(pl.multiple_of(here.group * QUART, QUART), QUART)
+    far_copies = [
+        copy_to(
+            far_quarter.at[m], gathered.at[3, m, own_quarter, pl.ds(HALF, HALF)],
+            far_sems.at[0, m], far_sems.at[1, m], to_partner,
+        )
+        for m in both
+    ]
     gain = norm_gain[pl.ds(here.pair, 1), pl.ds(pl.multiple_of(here.group * PART, PART), PART)]
     first_half = (1 - here.half).astype(F32)
 
@@ -397,6 +427,10 @@
     route_sum.start()
     for m in both:
         cut_in.start(m)
+    for m in both:
+        cut_cotan.start(m)
+    for m in both:
+        cut_in.pass_on(m)
     up_copy.start()
     for m in both:
         cut_in.take(m)
@@ -409,13 +443,15 @@
         scale = norm_scale(norm1[m].total_column())
         normed = (cut_in.value(m).astype(F32) * scale * gain).astype(BF16)
         go1[m].start(dot(marks(routes.by_slot(0, m)), normed))
+    for m in both:
+        cut_cotan.pass_on(m)
+    up_copy.wait_recv()
     down_copy.start()
-    for m in both:
-        cut_cotan.start(m)
-    up_copy.wait_recv()
     for m in both:
         rows1[m] = go1[m].take()
         up_parts(rows1.at[m], sum1[m])
+    for m in both:
+        sum1[m].pass_on()
     for m in both:
         cut_cotan.take(m)
         go_grads[m].start(exact_dot(weighted(routes.by_slot(1, m)), cut_cotan.value(m)))
@@ -436,6 +472,8 @@
         expert_out = back1[m].take()
         direct = cut_in.value(m).astype(F32) * first_half
         hand1[m].start(direct + exact_dot(weighted(routes.by_token(0, m)), expert_out))
+    for m in both:
+        sum_grads2[m].pass_on()
 
     for m in both:
         values = hand1[m].take().astype(F32)
@@ -446,6 +484,9 @@
     for m in both:
         rows2[m] = go2[m].take()
         up_parts(rows2.at[m], sum2[m])
+    rows_copy.start()
+    for m in both:
+        sum2[m].pass_on()
     for m in both:
         pre2[m] = sum2[m].total()
         all_pre_grad2[m].start(pre_gradient(sum_grads2[m].total(), pre2[m]))
@@ -461,7 +502,9 @@
     @pl.loop(0, PART // 128)
     def _(i):
         at = pl.ds(pl.multiple_of(i * 128, 128), 128)
-        sum_up[at] = t_dot(rows2[0, :, at], pre_grad2[0][...]) + t_dot(rows2[1, :, at], pre_grad2[1][...])
+        value = t_dot(rows2[0, :, at], pre_grad2[0][...]) + t_dot(rows2[1, :, at], pre_grad2[1][...])
+        sum_up[at] = value[:, 0:HALF]
+        give_up[at] = value[:, HALF:].astype(BF16)
 
     for m in both:
         scaled = dot(marks(routes.by_token(1, m)), back2[m].take()) * gain
@@ -483,9 +526,12 @@
     for m in both:
         incoming = hand2[m].take()
         go3[m].start(exact_dot(weighted(routes.by_slot(0, m)), incoming))
+    give_up_copy.start()
     for m in both:
         grads1[m] = go3[m].take()
         down_parts(grads1.at[m], sum_grads1[m])
+    for m in both:
+        sum_grads1[m].pass_on()
 
     @pl.loop(0, HALF // 128)
     def _(i):
@@ -496,7 +542,13 @@
 
     give_down_copy.start()
     for m in both:
-        all_pre_grad1[m].start(pre_gradient(sum_grads1[m].total(), pre1[m]))
+        quarter = pre_gradient(sum_grads1[m].total(), pre1[m])
+        far_quarter[m] = quarter[:, HALF:]
+        far_copies[m].start()
+        all_pre_grad1[m].start_near(quarter[:, 0:HALF])
+    for m in both:
+        far_copies[m].wait_recv()
+        all_pre_grad1[m].start_far()
     for m in both:
         all_pre_grad1[m].pass_on()
 
@@ -505,31 +557,25 @@
         at = pl.ds(pl.multiple_of(i * 128, 128), 128)
         sum_down[at] += t_dot(act1[0][:, at], grads1[0]) + t_dot(act1[1][:, at], grads1[1])
 
+    give_up_copy.wait_recv()
+    sum_up[...] += got_up[...].astype(F32)
+    rows_copy.wait_recv()
     for m in both:
         all_pre_grad1[m].wait_recv()
 
     @pl.loop(0, PART // 128)
     def _(i):
         at = pl.ds(pl.multiple_of(i * 128, 128), 128)
-        value = sum_up[at, HALF:]
+        value = sum_up[at]
         for m in both:
-            value = value + t_dot(rows1[m, :, at], pre_grad1[m][:, HALF:])
-        give_up[at] = value.astype(BF16)
-
-    give_up_copy.start()
-
-    @pl.loop(0, PART // 128)
-    def _(i):
-        at = pl.ds(pl.multiple_of(i * 128, 128), 128)
-        for m in both:
-            sum_up[at, 0:HALF] += t_dot(rows1[m, :, at], pre_grad1[m][:, 0:HALF])
+            value = value + t_dot(rows1[m, :, at], pre_grad1[m][:, 0:HALF])
+            value = value + t_dot(rows1_other[m, :, at], pre_grad1[m][:, HALF:])
+        grad_up[at] = value.astype(BF16)
 
     give_down_copy.wait_recv()
     grad_down[...] = (sum_down[0:HALF] + got_down[...].astype(F32)).astype(BF16)
-    give_up_copy.wait_recv()
-    grad_up[...] = (sum_up[:, 0:HALF] + got_up[...].astype(F32)).astype(BF16)
-
-    for sender in (cut_in, cut_cotan, route_sum, up_copy, down_copy, give_down_copy, give_up_copy):
+
+    for sender in (cut_in, cut_cotan, route_sum, up_copy, down_copy, give_down_copy, give_up_copy, rows_copy, *far_copies):
         sender.wait_send()
     for senders in (go1, back1, go_grads, go2, back2, go3, sum1, sum2, sum_grads2, sum_grads1, all_act1,
                     all_act2, all_pre_grad2, all_pre_grad1, norm1, norm2, mix, hand1, hand2):
@@ -567,16 +613,16 @@
     cut = vmem((BATCHES, GROUPS, BLOCK, PART), BF16)
     up_half, down_half = vmem((PART, HALF), BF16), vmem((HALF, PART), BF16)
     scratch = [
-        cut, cut, up_half, down_half,
+        cut, cut, cut, cut, up_half, down_half,
         vmem((3, 16, TOKENS), F32), vmem((16, TOKENS), F32), vmem((TOKENS, TOKENS), F32),
-        messages, messages, features, features, features, features,
-        hidden, vmem((4, BATCHES, 3, QUART, 2 * HALF), BF16), hidden, quarters, quarters,
+        messages, messages, features, features, features, features, features,
+        hidden, vmem((4, BATCHES, 6, QUART, HALF), BF16), hidden, quarters, quarters,
         vmem((3, BATCHES, 8, TOKENS), F32), vmem((3, BATCHES, 3, 8, TOKENS), F32), vmem((BATCHES, TOKENS, 1), F32),
         vmem((2, BATCHES, TOKENS, PART), BF16), vmem((2, BATCHES, 2, TOKENS, PART), BF16),
-        vmem((PART, 2 * HALF), F32), vmem((2 * HALF, PART), F32),
-        up_half, down_half, up_half, down_half,
-        dma((2, 2, BATCHES, 4)), dma((2, 4)), dma((2, 3)), dma((3, BATCHES, 2, 3)), dma((6, BATCHES, 2)),
-        dma((4, BATCHES, 2, 3)), dma((4, BATCHES, 2, 6)), dma((2, BATCHES, 2, 2)),
+        vmem((PART, HALF), F32), vmem((2 * HALF, PART), F32),
+        up_half, down_half, up_half, down_half, vmem((BATCHES, QUART, HALF), BF16),
+        dma((2, 2, 2, BATCHES, 3)), dma((2, 5)), dma((2, BATCHES)), dma((2, 3)), dma((3, BATCHES, 2, 3)), dma((6, BATCHES, 2)),
+        dma((4, BATCHES, 2, 6)), dma((4, BATCHES, 2, 6)), dma((2, BATCHES, 2, 2)),
     ]
     grad_up, grad_down = pl.pallas_call(
         update,

time: 369 us -> 324 us (0.88)
  Pallas kernels: 360 us -> 317 us
    pallas_call x1, Pallas kernels: 360 us -> 317 us  [local(): pl.pallas_call(update, out_shape=[jax.ShapeDtypeStruct((PART, HALF), BF16...]
where the time goes in v3:
time: 324 us; the launch traced here: 323 us
  Pallas kernels  317 us (98%)
  local copies, waits for them, and re-layouts  4.55 us (1%)
    pallas_call x1, Pallas kernels, local(): pl.pallas_call(update, out_shape=[jax.ShapeDtypeStruct((PART, HALF), BF16...  317 us

profile of v3, /device:TPU:6, one launch (start us, length us, event | category | flops | bytes accessed | tf_op | source)
XLA Modules:
  0.0 323.4 jit_solution(3856996856217388013)
XLA Ops:
  0.6 0.0 copy-start
  0.7 0.0 copy-start.2
  0.7 0.6 copy-done
  1.3 0.0 copy-done.2
  1.4 0.1 iota_compare_fusion
  1.5 0.1 copy.17
  1.6 0.1 eq.46
  1.7 0.2 convert_reduce_fusion
  1.9 0.1 reduce_sum.21
  2.1 0.1 fusion.7
  2.2 0.1 copy.19
  2.3 0.1 copy.18
  2.4 0.1 bitcast_divide_fusion
  2.5 0.1 copy.20
  2.6 0.1 tile.12
  2.7 0.6 broadcast_select_fusion.routes_own
  3.3 316.9 %shard_map.86 = (bf16[896,512]{1,0:T(8,128)(2,1)}, bf16[512,896]{1,0:T(8,128)(2,1)}) custom-call(bf16[2,2,32,896]{3,2,1,0:T(8,128)(2,1)} %stream.1, bf16[2,2,32,896]{3,2,1,0:T(8,128)(2,1)} %cotangent.1, bf16[896,512]{1,0:T(8,128)(2,1)} %bitcast.16, bf16[512,896]{1,0:T(8,128)(2,1)} %bitcast.17, f32[2,3584]{1,0:T(2,128)} %norm_gain.1, ...), custom_call_target="tpu_custom_call" | custom-call | tf_op jit(solution)/shard_map/pallas_call | solution.py:627
  320.2 0.0 copy-start.1
  320.2 2.2 copy.24
  322.5 0.0 copy-done.1
  322.5 0.9 copy.25
  (9 shorter events, 0.1 us)
Async XLA Ops:
  0.6 0.7 copy-start
  0.7 0.7 copy-start.2
  320.2 2.3 copy-start.1

commit v4 on v3

--- a/solution.py
+++ b/solution.py
@@ -447,57 +447,101 @@
         cut_cotan.pass_on(m)
     up_copy.wait_recv()
     down_copy.start()
-    for m in both:
+
+    def take_rows1(m):
         rows1[m] = go1[m].take()
         up_parts(rows1.at[m], sum1[m])
-    for m in both:
-        sum1[m].pass_on()
-    for m in both:
+
+    def start_grads2(m):
         cut_cotan.take(m)
         go_grads[m].start(exact_dot(weighted(routes.by_slot(1, m)), cut_cotan.value(m)))
-    for m in both:
+
+    def take_grads2(m):
+        grads2[m] = go_grads[m].take()
+        down_parts(grads2.at[m], sum_grads2[m])
+
+    def activate1(m):
         pre1[m] = sum1[m].total()
         all_act1[m].start(silu(pre1[m]).astype(BF16))
-    for m in both:
-        all_act1[m].pass_on()
-    down_copy.wait_recv()
-    for m in both:
+
+    def expert_out1(m):
         all_act1[m].wait_recv()
         act = act1[m]
         back1[m].start(dot(act[:, 0:HALF], down[...]) + dot(act[:, HALF:], down_other[...]))
-    for m in both:
-        grads2[m] = go_grads[m].take()
-        down_parts(grads2.at[m], sum_grads2[m])
-    for m in both:
+
+    def leave1(m):
         expert_out = back1[m].take()
         direct = cut_in.value(m).astype(F32) * first_half
         hand1[m].start(direct + exact_dot(weighted(routes.by_token(0, m)), expert_out))
-    for m in both:
-        sum_grads2[m].pass_on()
-
-    for m in both:
+
+    take_rows1(0)
+    sum1[0].pass_on()
+    start_grads2(0)
+    take_rows1(1)
+    activate1(0)
+    sum1[1].pass_on()
+    all_act1[0].pass_on()
+    down_copy.wait_recv()
+    expert_out1(0)
+    activate1(1)
+    all_act1[1].pass_on()
+    expert_out1(1)
+    take_grads2(0)
+    leave1(0)
+    sum_grads2[0].pass_on()
+    leave1(1)
+    start_grads2(1)
+
+    def arrive2(m):
         values = hand1[m].take().astype(F32)
         norm2[m].start_column(row_sum(values * values))
         scales[m] = norm_scale(norm2[m].total_column())
         normed = (hand1[m].again().astype(F32) * scales[m] * gain).astype(BF16)
         go2[m].start(dot(marks(routes.by_slot(1, m)), normed))
-    for m in both:
+
+    def take_rows2(m):
         rows2[m] = go2[m].take()
         up_parts(rows2.at[m], sum2[m])
-    rows_copy.start()
-    for m in both:
-        sum2[m].pass_on()
-    for m in both:
+
+    def activate2(m):
         pre2[m] = sum2[m].total()
         all_pre_grad2[m].start(pre_gradient(sum_grads2[m].total(), pre2[m]))
-    for m in both:
-        all_pre_grad2[m].pass_on()
-    for m in both:
+
+    def row_grads2(m):
         all_pre_grad2[m].wait_recv()
         grad = pre_grad2[m]
         back2[m].start(dot_t(grad[:, 0:HALF], up[...]) + dot_t(grad[:, HALF:], up_other[...]))
+
+    arrive2(0)
+    arrive2(1)
+    take_grads2(1)
+    rows_copy.start()
+    take_rows2(0)
+    sum_grads2[1].pass_on()
+    sum2[0].pass_on()
+    take_rows2(1)
+    activate2(0)
+    sum2[1].pass_on()
+    all_pre_grad2[0].pass_on()
+    row_grads2(0)
+    activate2(1)
+    all_pre_grad2[1].pass_on()
+    row_grads2(1)
+    def collect2(m):
+        scaled = dot(marks(routes.by_token(1, m)), back2[m].take()) * gain
+        mix[m].start_column(row_sum(hand1[m].again().astype(F32) * scaled))
+        return scaled
+
+    def leave2(m, scaled):
+        direct = cut_cotan.value(m).astype(F32) * first_half + scales[m] * scaled
+        mean = mix[m].total_column() * (1.0 / (GROUPS * PART))
+        scale = scales[m]
+        hand2[m].start(direct - hand1[m].again().astype(F32) * (scale * scale * scale * mean))
+
+    scaled = collect2(0)
     for m in both:
         all_act2[m].start(silu(pre2[m]).astype(BF16))
+    leave2(0, scaled)
 
     @pl.loop(0, PART // 128)
     def _(i):
@@ -506,32 +550,45 @@
         sum_up[at] = value[:, 0:HALF]
         give_up[at] = value[:, HALF:].astype(BF16)
 
-    for m in both:
-        scaled = dot(marks(routes.by_token(1, m)), back2[m].take()) * gain
-        mix[m].start_column(row_sum(hand1[m].again().astype(F32) * scaled))
-        direct = cut_cotan.value(m).astype(F32) * first_half + scales[m] * scaled
-        mean = mix[m].total_column() * (1.0 / (GROUPS * PART))
-        scale = scales[m]
-        hand2[m].start(direct - hand1[m].again().astype(F32) * (scale * scale * scale * mean))
+    scaled = collect2(1)
     for m in both:
         all_act2[m].pass_on()
+    leave2(1, scaled)
     for m in both:
         all_act2[m].wait_recv()
+
+    def arrive1(m):
+        go3[m].start(exact_dot(weighted(routes.by_slot(0, m)), hand2[m].take()))
+
+    arrive1(0)
 
     @pl.loop(0, 2 * HALF // 128)
     def _(i):
         at = pl.ds(pl.multiple_of(i * 128, 128), 128)
         sum_down[at] = t_dot(act2[0][:, at], grads2[0]) + t_dot(act2[1][:, at], grads2[1])
 
-    for m in both:
-        incoming = hand2[m].take()
-        go3[m].start(exact_dot(weighted(routes.by_slot(0, m)), incoming))
+    arrive1(1)
     give_up_copy.start()
-    for m in both:
+    def take_grads1(m):
         grads1[m] = go3[m].take()
         down_parts(grads1.at[m], sum_grads1[m])
-    for m in both:
-        sum_grads1[m].pass_on()
+
+    def pre_grads1(m):
+        quarter = pre_gradient(sum_grads1[m].total(), pre1[m])
+        far_quarter[m] = quarter[:, HALF:]
+        far_copies[m].start()
+        all_pre_grad1[m].start_near(quarter[:, 0:HALF])
+
+    def far_pre_grads1(m):
+        far_copies[m].wait_recv()
+        all_pre_grad1[m].start_far()
+
+    take_grads1(0)
+    sum_grads1[0].pass_on()
+    take_grads1(1)
+    pre_grads1(0)
+    sum_grads1[1].pass_on()
+    far_pre_grads1(0)
 
     @pl.loop(0, HALF // 128)
     def _(i):
@@ -540,17 +597,11 @@
         value = sum_down[far] + t_dot(act1[0][:, far], grads1[0]) + t_dot(act1[1][:, far], grads1[1])
         give_down[at] = value.astype(BF16)
 
+    pre_grads1(1)
     give_down_copy.start()
-    for m in both:
-        quarter = pre_gradient(sum_grads1[m].total(), pre1[m])
-        far_quarter[m] = quarter[:, HALF:]
-        far_copies[m].start()
-        all_pre_grad1[m].start_near(quarter[:, 0:HALF])
-    for m in both:
-        far_copies[m].wait_recv()
-        all_pre_grad1[m].start_far()
-    for m in both:
-        all_pre_grad1[m].pass_on()
+    all_pre_grad1[0].pass_on()
+    far_pre_grads1(1)
+    all_pre_grad1[1].pass_on()
 
     @pl.loop(0, HALF // 128)
     def _(i):

time: 324 us -> 307 us (0.948)
  Pallas kernels: 317 us -> 299 us
    pallas_call x1, Pallas kernels: 317 us -> 299 us  [local(): pl.pallas_call(update, out_shape=[jax.ShapeDtypeStruct((PART, HALF), BF16...]
where the time goes in v4:
time: 307 us; the launch traced here: 305 us
  Pallas kernels  299 us (97%)
  local copies, waits for them, and re-layouts  4.55 us (1%)
    pallas_call x1, Pallas kernels, local(): pl.pallas_call(update, out_shape=[jax.ShapeDtypeStruct((PART, HALF), BF16...  299 us

profile of v4, /device:TPU:6, one launch (start us, length us, event | category | flops | bytes accessed | tf_op | source)
XLA Modules:
  0.0 305.0 jit_solution(17897979037101736396)
XLA Ops:
  0.6 0.0 copy-start
  0.7 0.0 copy-start.2
  0.7 0.6 copy-done
  1.3 0.0 copy-done.2
  1.4 0.1 iota_compare_fusion
  1.5 0.1 copy.17
  1.6 0.1 eq.46
  1.7 0.2 convert_reduce_fusion
  1.9 0.1 reduce_sum.21
  2.1 0.1 fusion.7
  2.2 0.1 copy.19
  2.3 0.1 copy.18
  2.4 0.1 bitcast_divide_fusion
  2.5 0.1 copy.20
  2.6 0.1 tile.12
  2.7 0.6 broadcast_select_fusion.routes_own
  3.3 298.5 %shard_map.86 = (bf16[896,512]{1,0:T(8,128)(2,1)}, bf16[512,896]{1,0:T(8,128)(2,1)}) custom-call(bf16[2,2,32,896]{3,2,1,0:T(8,128)(2,1)} %stream.1, bf16[2,2,32,896]{3,2,1,0:T(8,128)(2,1)} %cotangent.1, bf16[896,512]{1,0:T(8,128)(2,1)} %bitcast.16, bf16[512,896]{1,0:T(8,128)(2,1)} %bitcast.17, f32[2,3584]{1,0:T(2,128)} %norm_gain.1, ...), custom_call_target="tpu_custom_call" | custom-call | tf_op jit(solution)/shard_map/pallas_call | solution.py:678
  301.9 0.0 copy-start.1
  301.9 2.2 copy.24
  304.1 0.0 copy-done.1
  304.1 0.9 copy.25
  (9 shorter events, 0.1 us)
Async XLA Ops:
  0.6 0.7 copy-start
  0.7 0.7 copy-start.2
  301.9 2.3 copy-start.1

commit v5 on v4

--- a/solution.py
+++ b/solution.py
@@ -84,7 +84,7 @@
         )
 
     def start(self, rows):
-        messages = rows.reshape(EXPERTS, MSG, PART).astype(BF16)
+        messages = rows.astype(BF16).reshape(EXPERTS, MSG, PART)
         self.src[...] = messages
         self.dst[0:1] = messages[0:1]
 
@@ -96,7 +96,7 @@
 
     def take(self):
         self.copy(1, EXPERTS - 1).wait_recv()
-        return self.dst[...].astype(F32).reshape(SLOTS, PART).astype(BF16)
+        return self.dst[...].reshape(SLOTS, PART)
 
     def wait_send(self):
         self.copy(1, EXPERTS - 1).wait_send()
@@ -439,10 +439,11 @@
     total = route_sum.total()
     routes_rows[...] = total
     routes_columns[...] = jnp.concatenate([total] * (TOKENS // total.shape[0]), axis=0).T
+    spreads = [marks(routes.by_slot(0, m)) for m in both]
     for m in both:
         scale = norm_scale(norm1[m].total_column())
         normed = (cut_in.value(m).astype(F32) * scale * gain).astype(BF16)
-        go1[m].start(dot(marks(routes.by_slot(0, m)), normed))
+        go1[m].start(dot(spreads[m], normed))
     for m in both:
         cut_cotan.pass_on(m)
     up_copy.wait_recv()
@@ -470,9 +471,9 @@
         back1[m].start(dot(act[:, 0:HALF], down[...]) + dot(act[:, HALF:], down_other[...]))
 
     def leave1(m):
-        expert_out = back1[m].take()
+        weights = weighted(routes.by_token(0, m))
         direct = cut_in.value(m).astype(F32) * first_half
-        hand1[m].start(direct + exact_dot(weighted(routes.by_token(0, m)), expert_out))
+        hand1[m].start(direct + exact_dot(weights, back1[m].take()))
 
     take_rows1(0)
     sum1[0].pass_on()
@@ -495,9 +496,10 @@
     def arrive2(m):
         values = hand1[m].take().astype(F32)
         norm2[m].start_column(row_sum(values * values))
+        spread = marks(routes.by_slot(1, m))
         scales[m] = norm_scale(norm2[m].total_column())
         normed = (hand1[m].again().astype(F32) * scales[m] * gain).astype(BF16)
-        go2[m].start(dot(marks(routes.by_slot(1, m)), normed))
+        go2[m].start(dot(spread, normed))
 
     def take_rows2(m):
         rows2[m] = go2[m].take()
@@ -528,7 +530,8 @@
     all_pre_grad2[1].pass_on()
     row_grads2(1)
     def collect2(m):
-        scaled = dot(marks(routes.by_token(1, m)), back2[m].take()) * gain
+        collect = marks(routes.by_token(1, m))
+        scaled = dot(collect, back2[m].take()) * gain
         mix[m].start_column(row_sum(hand1[m].again().astype(F32) * scaled))
         return scaled
 
@@ -558,7 +561,8 @@
         all_act2[m].wait_recv()
 
     def arrive1(m):
-        go3[m].start(exact_dot(weighted(routes.by_slot(0, m)), hand2[m].take()))
+        weights = weighted(routes.by_slot(0, m))
+        go3[m].start(exact_dot(weights, hand2[m].take()))
 
     arrive1(0)
 
@@ -611,17 +615,23 @@
     give_up_copy.wait_recv()
     sum_up[...] += got_up[...].astype(F32)
     rows_copy.wait_recv()
-    for m in both:
-        all_pre_grad1[m].wait_recv()
+    def rows_grads1(m, at):
+        own = t_dot(rows1[m, :, at], pre_grad1[m][:, 0:HALF])
+        return own + t_dot(rows1_other[m, :, at], pre_grad1[m][:, HALF:])
+
+    all_pre_grad1[0].wait_recv()
 
     @pl.loop(0, PART // 128)
     def _(i):
         at = pl.ds(pl.multiple_of(i * 128, 128), 128)
-        value = sum_up[at]
-        for m in both:
-            value = value + t_dot(rows1[m, :, at], pre_grad1[m][:, 0:HALF])
-            value = value + t_dot(rows1_other[m, :, at], pre_grad1[m][:, HALF:])
-        grad_up[at] = value.astype(BF16)
+        sum_up[at] += rows_grads1(0, at)
+
+    all_pre_grad1[1].wait_recv()
+
+    @pl.loop(0, PART // 128)
+    def _(i):
+        at = pl.ds(pl.multiple_of(i * 128, 128), 128)
+        grad_up[at] = (sum_up[at] + rows_grads1(1, at)).astype(BF16)
 
     give_down_copy.wait_recv()
     grad_down[...] = (sum_down[0:HALF] + got_down[...].astype(F32)).astype(BF16)

time: 307 us -> 311 us (1.013)
  the two profiles are of different devices: /device:TPU:6 before, /device:TPU:2 now
where the time goes in v5:
time: 311 us
  Pallas kernels  304 us (98%)
  local copies, waits for them, and re-layouts  4.55 us (1%)
    pallas_call x1, Pallas kernels, local(): pl.pallas_call(update, out_shape=[jax.ShapeDtypeStruct((PART, HALF), BF16...  304 us

profile of v5, /device:TPU:2, one launch (start us, length us, event | category | flops | bytes accessed | tf_op | source)
XLA Modules:
  0.0 310.9 jit_solution(9682914025597820)
XLA Ops:
  0.6 0.0 copy-start
  0.7 0.0 copy-start.2
  0.7 0.6 copy-done
  1.3 0.0 copy-done.2
  1.4 0.1 iota_compare_fusion
  1.5 0.1 copy.17
  1.6 0.1 eq.46
  1.7 0.2 convert_reduce_fusion
  1.9 0.1 reduce_sum.21
  2.1 0.1 fusion.7
  2.2 0.1 copy.19
  2.3 0.1 copy.18
  2.4 0.1 bitcast_divide_fusion
  2.5 0.1 copy.20
  2.6 0.1 tile.12
  2.7 0.6 broadcast_select_fusion.routes_own
  3.3 304.4 %shard_map.86 = (bf16[896,512]{1,0:T(8,128)(2,1)}, bf16[512,896]{1,0:T(8,128)(2,1)}) custom-call(bf16[2,2,32,896]{3,2,1,0:T(8,128)(2,1)} %stream.1, bf16[2,2,32,896]{3,2,1,0:T(8,128)(2,1)} %cotangent.1, bf16[896,512]{1,0:T(8,128)(2,1)} %bitcast.16, bf16[512,896]{1,0:T(8,128)(2,1)} %bitcast.17, f32[2,3584]{1,0:T(2,128)} %norm_gain.1, ...), custom_call_target="tpu_custom_call" | custom-call | tf_op jit(solution)/shard_map/pallas_call | solution.py:688
  307.7 0.0 copy-start.1
  307.7 2.2 copy.24
  310.0 0.0 copy-done.1
  310.0 0.9 copy.25
  (9 shorter events, 0.1 us)
Async XLA Ops:
  0.6 0.7 copy-start
  0.7 0.7 copy-start.2
  307.7 2.3 copy-start.1
